TPU v7x, 128 devices: a whole 4x4x4 slice. The times are simulated.
128 devices in a mesh: seq: 8 (over x, y_hi), head: 16 (over z, y_lo, core).
Axes of the slice: x: 4, y: 4 (y_hi: 2, y_lo: 2; y = y_hi * 2 + y_lo), z: 4, core: 2. Of those that a mesh axis runs over, the one named last changes fastest.
Arguments:
- token_ids: int32 [131072], P(('seq', 'head')), may hold values from 0 to 511
- bar_mask: int32 [131072], P(('seq', 'head')), may hold values from 0 to 1, as said below
- embed: bfloat16 [512, 1024], replicated, may hold values from -6 to 6
- mask_embed: bfloat16 [1024], replicated, may hold values from -6 to 6
- local_gain: bfloat16 [1024], replicated, may hold values from 0.25 to 1.75
- local_query: bfloat16 [1024, 1024], replicated, may hold values from -100 to 100
- local_key: bfloat16 [1024, 1024], replicated, may hold values from -1 to 1
- local_value: bfloat16 [1024, 1024], replicated, may hold values from -0.1875 to 0.1875
- local_out: bfloat16 [1024, 1024], replicated, may hold values from -0.1875 to 0.1875
- coarse_gain: bfloat16 [1024], replicated, may hold values from 0.25 to 1.75
- coarse_query: bfloat16 [1024, 1024], replicated, may hold values from -100 to 100
- coarse_key: bfloat16 [1024, 1024], replicated, may hold values from -1 to 1
- coarse_value: bfloat16 [1024, 1024], replicated, may hold values from -0.1875 to 0.1875
- coarse_out: bfloat16 [1024, 1024], replicated, may hold values from -0.1875 to 0.1875
Outputs:
- block_out: bfloat16 [131072, 1024], P(('seq', 'head'))
Inputs may be any that keep to these rules, and one draw needn't show every extreme that they name: bar_mask is constant on each bar, a run of 1 to 96 consecutive tokens.
All inputs are finite; a program needn't handle non-finite values.
Results may differ from a plain program's by a relative error of at most 0.024.
Values may be sent and summed in bfloat16 or wider, within the bound.
No kernel may reach another device: no remote copies, remote signals or barrier semaphores. Data moves between devices by JAX's collectives and lax.ppermute only.
A program may use at most 192 MiB of HBM per device.

v0:
```python
import jax
import jax.numpy as jnp
from jax import lax
from jax.sharding import PartitionSpec as P

HEADS = 16
HALF_WIN = 512
POOL = 64


def with_halo(block, sides, width):
    for axis, dim in sides:
        count = lax.axis_size(axis)
        forward = [(i, i + 1) for i in range(count - 1)]
        backward = [(target, source) for source, target in forward]
        low = lax.ppermute(
            lax.slice_in_dim(block, block.shape[dim] - width, None, axis=dim), axis, forward
        )
        high = lax.ppermute(lax.slice_in_dim(block, 0, width, axis=dim), axis, backward)
        block = jnp.concatenate([low, block, high], axis=dim)
    return block


def normalize(rows, gain):
    wide = rows.astype(jnp.float32)
    scaled = wide * lax.rsqrt(jnp.mean(wide * wide, axis=-1, keepdims=True) + 1e-05)
    return (scaled * gain.astype(jnp.float32)).astype(jnp.bfloat16)


def project(rows, weight):
    return jnp.dot(rows, weight, preferred_element_type=jnp.float32).astype(jnp.bfloat16)


def local_block(q_rows, k_rows, v_rows, q_start, k_start, total, reach):
    count = q_rows.shape[0]
    span = k_rows.shape[0]
    width = q_rows.shape[1] // HEADS
    qh = q_rows.reshape(count, HEADS, width)
    kh = k_rows.reshape(span, HEADS, width)
    vh = v_rows.reshape(span, HEADS, width)
    scores = jnp.einsum("qhd,khd->hqk", qh, kh, preferred_element_type=jnp.float32) * width ** (
        -0.5
    )
    q_pos = q_start + jnp.arange(count, dtype=jnp.int32)
    k_pos = k_start + jnp.arange(span, dtype=jnp.int32)
    valid = (
        (jnp.abs(q_pos[:, None] - k_pos[None, :]) <= reach)
        & (k_pos[None, :] >= 0)
        & (k_pos[None, :] < total)
    )
    scores = jnp.where(valid[None], scores, -1e30)
    top = jnp.max(scores, axis=-1, keepdims=True)
    probs = jnp.exp(scores - top)
    probs = (probs / jnp.sum(probs, axis=-1, keepdims=True)).astype(jnp.bfloat16)
    mixed = jnp.einsum("hqk,khd->qhd", probs, vh, preferred_element_type=jnp.float32)
    return mixed.reshape(count, HEADS * width).astype(jnp.bfloat16)


def body(
    token_ids,
    bar_mask,
    embed,
    mask_embed,
    local_gain,
    local_query,
    local_key,
    local_value,
    local_out,
    coarse_gain,
    coarse_query,
    coarse_key,
    coarse_value,
    coarse_out,
):
    inputs = jnp.where(
        bar_mask[:, None] == 1, mask_embed[None, :], jnp.take(embed, token_ids, axis=0)
    )
    normed = normalize(inputs, local_gain)
    queries = project(normed, local_query)
    width = inputs.shape[1]
    both = jnp.concatenate([project(normed, local_key), project(normed, local_value)], axis=1)
    both_ext = with_halo(both, ((("seq", "head"), 0),), HALF_WIN)
    keys_ext = both_ext[:, :width]
    values_ext = both_ext[:, width:]
    rows = inputs.shape[0]
    block = min(512, rows)
    offset = lax.axis_index(("seq", "head")) * rows
    total = rows * lax.axis_size("seq") * lax.axis_size("head")

    def one_block(index):
        first = index * block
        q_rows = lax.dynamic_slice_in_dim(queries, first, block, 0)
        k_rows = lax.dynamic_slice_in_dim(keys_ext, first, block + 2 * HALF_WIN, 0)
        v_rows = lax.dynamic_slice_in_dim(values_ext, first, block + 2 * HALF_WIN, 0)
        return local_block(
            q_rows, k_rows, v_rows, offset + first, offset + first - HALF_WIN, total, HALF_WIN
        )

    local_att = lax.map(one_block, jnp.arange(rows // block, dtype=jnp.int32)).reshape(rows, width)
    mid = (
        inputs.astype(jnp.float32)
        + jnp.dot(local_att, local_out, preferred_element_type=jnp.float32)
    ).astype(jnp.bfloat16)
    pooled = jnp.mean(mid.astype(jnp.float32).reshape(rows // POOL, POOL, width), axis=1).astype(
        jnp.bfloat16
    )
    coarse_normed = normalize(pooled, coarse_gain)
    cq = project(coarse_normed, coarse_query)
    ck = project(coarse_normed, coarse_key)
    cv = project(coarse_normed, coarse_value)
    head_q, head_k, head_v = (
        lax.all_to_all(cq, "head", split_axis=1, concat_axis=0, tiled=True),
        lax.all_to_all(ck, "head", split_axis=1, concat_axis=0, tiled=True),
        lax.all_to_all(cv, "head", split_axis=1, concat_axis=0, tiled=True),
    )
    size_head = width // HEADS
    local_heads = head_q.shape[1] // size_head
    count = head_q.shape[0]
    scale = size_head ** (-0.5)
    qh = head_q.reshape(count, local_heads, size_head)
    running = jnp.full((local_heads, count), -1e30, jnp.float32)
    part_k = lax.all_gather(head_k, "seq", axis=0, tiled=True)
    part_v = lax.all_gather(head_v, "seq", axis=0, tiled=True)
    span = part_k.shape[0]
    kh = part_k.reshape(span, local_heads, size_head)
    vh = part_v.reshape(span, local_heads, size_head).astype(jnp.float32)
    scores = jnp.einsum("qhd,khd->hqk", qh, kh, preferred_element_type=jnp.float32) * scale
    newest = jnp.maximum(running, jnp.max(scores, axis=-1))
    probs = jnp.exp(scores - newest[..., None])
    total_w = jnp.sum(probs, axis=-1)
    accum = jnp.einsum("hqk,khd->hqd", probs, vh, precision=lax.Precision.HIGHEST)
    running, total_w, accum = (newest, total_w, accum)
    mixed = (accum / total_w[..., None]).transpose(1, 0, 2)
    coarse_att = mixed.reshape(count, local_heads * size_head).astype(jnp.bfloat16)
    back = lax.all_to_all(coarse_att, "head", split_axis=0, concat_axis=1, tiled=True)
    lifted = jnp.dot(back, coarse_out, preferred_element_type=jnp.float32)
    return (mid.astype(jnp.float32) + jnp.repeat(lifted, POOL, axis=0)).astype(jnp.bfloat16)


def solution(mesh):
    placed = (
        P(("seq", "head")),
        P(("seq", "head")),
        P(),
        P(),
        P(),
        P(),
        P(),
        P(),
        P(),
        P(),
        P(),
        P(),
        P(),
        P(),
    )
    return jax.shard_map(
        body, mesh=mesh, in_specs=placed, out_specs=P(("seq", "head"), None), check_vma=False
    )
```

profile of v0, /device:TPU:0, one launch (start us, length us, event | category | flops | bytes accessed | tf_op | source)
XLA Modules:
  0.0 342.7 jit_solution(11156251871380018920)
XLA Ops:
  0.0 0.8 fusion.30
  0.8 0.7 compare_and_fusion
  1.6 7.4 %gather_fusion = bf16[1024,1024]{1,0:T(8,128)(2,1)} fusion(bf16[512,1024]{1,0:T(8,128)(2,1)} %param.18, s32[1024]{0:T(1024)S(1)} %fusion.30), kind=kCustom, calls=%fused_computation | custom fusion | bytes 4198400 | tf_op jit(solution)/shard_map/jit(_take)/gather | solution.py:76
  9.0 2.7 fusion.15
  11.7 5.2 %convolution_convert_fusion.1 = bf16[1024,1024]{0,1:T(8,128)(2,1)S(1)} fusion(bf16[1024,1024]{1,0:T(8,128)(2,1)} %param.23, f32[1024]{0:T(1024)S(1)} %convert_element_type.84, f32[1024]{0:T(1024)S(1)} %add_rsqrt_fusion, bf16[1024,1024]{1,0:T(8,128)(2,1)S(1)} %copy-done.2, pred[1024]{0:T(1024)(128)(4,1)S(1)} %get-tuple-element.144, ...), kind=kOutput, calls=%fused_computation.45 | convolution fusion | flops 2154823680 | bytes 6303744 | tf_op jit(solution)/shard_map/dot_general | solution.py:31
  16.9 3.5 %convolution_convert_fusion.2 = bf16[1024,1024]{0,1:T(8,128)(2,1)S(1)} fusion(bf16[1024,1024]{1,0:T(8,128)(2,1)S(1)} %copy-done.19, f32[1024]{0:T(1024)S(1)} %convert_element_type.84, f32[1024]{0:T(1024)S(1)} %add_rsqrt_fusion, bf16[1024,1024]{1,0:T(8,128)(2,1)S(1)} %copy-done.2, pred[1024]{0:T(1024)(128)(4,1)S(1)} %get-tuple-element.144, ...), kind=kOutput, calls=%fused_computation.46 | convolution fusion | flops 2154823680 | bytes 6303744 | tf_op jit(solution)/shard_map/dot_general | solution.py:31
  20.4 5.5 %fusion.20 = (bf16[512,2048]{0,1:T(8,128)(2,1)}, bf16[512,2048]{0,1:T(8,128)(2,1)}) fusion(bf16[1024,1024]{0,1:T(8,128)(2,1)S(1)} %convolution_convert_fusion.2, bf16[1024,1024]{0,1:T(8,128)(2,1)S(1)} %convolution_convert_fusion.1), kind=kLoop, calls=%fused_computation.39 | loop fusion | flops 8388608 | bytes 8388608 | tf_op jit(solution)/shard_map/concatenate | solution.py:81
  25.9 2.6 collective-permute-start
  28.5 1.5 collective-permute-start.1
  30.6 6.2 %convolution_convert_fusion = bf16[1024,1024]{1,0:T(8,128)(2,1)} fusion(bf16[1024,1024]{1,0:T(8,128)(2,1)} %param.21, f32[1024]{0:T(1024)S(1)} %convert_element_type.84, f32[1024]{0:T(1024)S(1)} %add_rsqrt_fusion, bf16[1024,1024]{1,0:T(8,128)(2,1)} %gather_fusion, pred[1024]{0:T(1024)(128)(4,1)S(1)} %get-tuple-element.144, ...), kind=kOutput, calls=%fused_computation.44 | convolution fusion | flops 2154823680 | bytes 6303744 | tf_op jit(solution)/shard_map/dot_general | solution.py:31
  36.9 20.3 %pad_maximum_fusion = bf16[2048,2048]{0,1:T(8,128)(2,1)S(1)} fusion(bf16[512,2048]{0,1:T(8,128)(2,1)} %collective-permute-done.1, bf16[1024,1024]{0,1:T(8,128)(2,1)S(1)} %copy-done.5, bf16[1024,1024]{0,1:T(8,128)(2,1)S(1)} %copy-done.7, bf16[512,2048]{0,1:T(8,128)(2,1)} %collective-permute-done), kind=kLoop, calls=%fused_computation.25 | loop fusion | flops 33554432 | bytes 16777216 | tf_op jit(solution)/shard_map/concatenate | solution.py:20
  57.2 3.8 %fusion.35 = (bf16[2048,1024]{0,1:T(8,128)(2,1)}, bf16[2048,1024]{0,1:T(8,128)(2,1)}) fusion(bf16[2048,2048]{0,1:T(8,128)(2,1)S(1)} %pad_maximum_fusion), kind=kLoop, calls=%fused_computation.69 | loop fusion | bytes 16777216 | tf_op jit(solution)/shard_map/slice | solution.py:83
  61.0 114.7 %while.12 = (s32[]{:T(128)}, bf16[2,512,1024]{2,1,0:T(8,128)(2,1)}, s32[2]{0:T(128)S(1)}, bf16[2048,1024]{0,1:T(8,128)(2,1)}, s32[]{:T(128)}, /*index=5*/bf16[10...) while((s32[]{:T(128)}, bf16[2,512,1024]{2,1,0:T(8,128)(2,1)}, ...), condition=%wide.region_4.5_spmd, body=%wide.region_1.4_spmd.sunk | while | flops 3301187584 | bytes 131685120 | solution.py:99
  61.2 0.7 dynamic_slice.33
  62.6 2.0 fusion.70
  64.6 5.9 %constant_dynamic-slice_fusion.5 = (bf16[1536,1024]{0,1:T(8,128)(2,1)}, bf16[1536,1024]{0,1:T(8,128)(2,1)}) fusion(bf16[2048,1024]{0,1:T(8,128)(2,1)} %get-tuple-element.233, s32[]{:T(128)S(6)} %select_n.87, bf16[2048,1024]{0,1:T(8,128)(2,1)} %get-tuple-element.230), kind=kLoop, calls=%fused_computation.19.clone.1 | loop fusion | bytes 12582916 | tf_op jit(solution)/shard_map/while/body/eval_jaxpr/dynamic_slice | solution.py:93
  70.4 1.3 constant_dynamic-slice_fusion.6
  71.7 1.3 copy.41
  73.1 23.1 %fusion.71 = (f32[16,512]{1,0:T(8,128)S(1)}, f32[16,512,1536]{2,1,0:T(8,128)}) fusion(pred[512,1536]{1,0:T(8,128)(4,1)} %fusion.70, bf16[512,16,64]{0,2,1:T(8,128)(2,1)} %bitcast.76, bf16[1536,16,64]{0,2,1:T(8,128)(2,1)} %bitcast.75), kind=kOutput, calls=%fused_computation.68.clone.1 | convolution fusion | flops 1660945920 | bytes 55345152 | tf_op jit(solution)/shard_map/while/body/eval_jaxpr/sub | solution.py:53
  96.1 19.8 %fusion.72 = bf16[16,64,512]{2,1,0:T(8,128)(2,1)} fusion(bf16[1536,16,64]{0,2,1:T(8,128)(2,1)} %bitcast.74, f32[16,512,1536]{2,1,0:T(8,128)} %get-tuple-element.199, f32[16,512]{1,0:T(8,128)S(1)} %get-tuple-element.200), kind=kOutput, calls=%fused_computation.13.clone.1 | convolution fusion | flops 1636302848 | bytes 54558720 | tf_op jit(solution)/shard_map/while/body/eval_jaxpr/hqk,khd->qhd/dot_general | solution.py:55
  115.9 1.5 copy.42
  117.4 1.1 constant_dynamic-update-slice_fusion.2
  119.8 2.0 fusion.70
  121.8 5.9 %constant_dynamic-slice_fusion.5 = (bf16[1536,1024]{0,1:T(8,128)(2,1)}, bf16[1536,1024]{0,1:T(8,128)(2,1)}) fusion(bf16[2048,1024]{0,1:T(8,128)(2,1)} %get-tuple-element.233, s32[]{:T(128)S(6)} %select_n.87, bf16[2048,1024]{0,1:T(8,128)(2,1)} %get-tuple-element.230), kind=kLoop, calls=%fused_computation.19.clone.1 | loop fusion | bytes 12582916 | tf_op jit(solution)/shard_map/while/body/eval_jaxpr/dynamic_slice | solution.py:93
  127.7 1.3 constant_dynamic-slice_fusion.6
  129.0 1.3 copy.41
  130.3 23.1 %fusion.71 = (f32[16,512]{1,0:T(8,128)S(1)}, f32[16,512,1536]{2,1,0:T(8,128)}) fusion(pred[512,1536]{1,0:T(8,128)(4,1)} %fusion.70, bf16[512,16,64]{0,2,1:T(8,128)(2,1)} %bitcast.76, bf16[1536,16,64]{0,2,1:T(8,128)(2,1)} %bitcast.75), kind=kOutput, calls=%fused_computation.68.clone.1 | convolution fusion | flops 1660945920 | bytes 55345152 | tf_op jit(solution)/shard_map/while/body/eval_jaxpr/sub | solution.py:53
  153.4 19.8 %fusion.72 = bf16[16,64,512]{2,1,0:T(8,128)(2,1)} fusion(bf16[1536,16,64]{0,2,1:T(8,128)(2,1)} %bitcast.74, f32[16,512,1536]{2,1,0:T(8,128)} %get-tuple-element.199, f32[16,512]{1,0:T(8,128)S(1)} %get-tuple-element.200), kind=kOutput, calls=%fused_computation.13.clone.1 | convolution fusion | flops 1636302848 | bytes 54558720 | tf_op jit(solution)/shard_map/while/body/eval_jaxpr/hqk,khd->qhd/dot_general | solution.py:55
  173.1 1.5 copy.42
  174.6 1.1 constant_dynamic-update-slice_fusion.2
  175.8 6.9 %bitcast_reduce_fusion = (f32[16,1024]{1,0:T(8,128)S(1)}, f32[1024,1024]{1,0:T(8,128)}) fusion(bf16[1024,1024]{1,0:T(8,128)(2,1)} %gather_fusion, pred[1024]{0:T(1024)(128)(4,1)S(1)} %copy-done.12, bf16[1024]{0:T(1024)(128)(2,1)S(1)} %copy-done.16, pred[1024]{0:T(1024)(128)(4,1)S(1)} %copy-done.14, bf16[1024,1024]{1,0:T(8,128)(2,1)} %bitcast.86, ...), kind=kOutput, calls=%fused_computation.37 | convolution fusion | flops 2154807296 | bytes 10555392 | tf_op jit(solution)/shard_map/dot_general | solution.py:102
  183.4 0.7 reshape.217
  184.2 46.0 %all-to-all-start.1 = ((bf16[16,2,512]{2,1,0:T(2,128)(2,1)}), bf16[16,2,512]{2,1,0:T(2,128)(2,1)S(1)}, u32[]{:S(2)}, u32[]{:S(2)}) async-start(bf16[16,2,512]{2,1,0:T(2,128)(2,1)} %reshape.217), calls=%async_computation.1 | async-start | bytes 65536 | tf_op jit(solution)/shard_map/all_to_all | solution.py:113
  230.2 2.1 convolution_convert_fusion.5
  232.9 0.7 reshape.215
  233.8 0.7 reshape.213
  234.5 1.8 all-to-all-done.1
  236.3 3.9 %all-to-all-start = ((bf16[16,2,512]{2,1,0:T(2,128)(2,1)}), bf16[16,2,512]{2,1,0:T(2,128)(2,1)S(1)}, u32[]{:S(2)}, u32[]{:S(2)}) async-start(bf16[16,2,512]{2,1,0:T(2,128)(2,1)} %reshape.215), calls=%async_computation | async-start | bytes 65536 | tf_op jit(solution)/shard_map/all_to_all | solution.py:112
  240.3 35.0 %all_gather.6 = bf16[2048,64]{1,0:T(8,128)(2,1)S(1)} all-gather(bf16[256,64]{1,0:T(8,128)(2,1)S(1)} %bitcast.79), channel_id=1, replica_groups=mesh['seq'=8,'head'=16] {'seq'}, dimensions={0}, use_global_device_ids=true | all-gather | bytes 294912 | tf_op jit(solution)/shard_map/all_gather | solution.py:122
  275.4 6.0 %all-to-all-start.2 = ((bf16[16,2,512]{2,1,0:T(2,128)(2,1)}), bf16[16,2,512]{2,1,0:T(2,128)(2,1)S(1)}, u32[]{:S(2)}, u32[]{:S(2)}) async-start(bf16[16,2,512]{2,1,0:T(2,128)(2,1)} %reshape.213), calls=%async_computation.2 | async-start | bytes 65536 | tf_op jit(solution)/shard_map/all_to_all | solution.py:114
  281.5 1.8 fusion.36
  283.3 4.2 %all-to-all-done.2 = bf16[16,2,512]{2,1,0:T(2,128)(2,1)S(1)} async-done(((bf16[16,2,512]{2,1,0:T(2,128)(2,1)}), bf16[16,2,512]{2,1,0:T(2,128)(2,1)S(1)}, u32[]{:S(2)}, u32[]{:S(2)}) %all-to-all-start.2) | async-done | bytes 32800 | tf_op jit(solution)/shard_map/all_to_all | solution.py:114
  287.6 35.0 %all_gather.7 = bf16[2048,64]{1,0:T(8,128)(2,1)S(1)} all-gather(bf16[256,64]{1,0:T(8,128)(2,1)S(1)} %bitcast.80), channel_id=1, replica_groups=mesh['seq'=8,'head'=16] {'seq'}, dimensions={0}, use_global_device_ids=true | all-gather | bytes 294912 | tf_op jit(solution)/shard_map/all_gather | solution.py:123
  322.6 2.0 fusion.22
  324.6 1.5 fusion.25
  326.3 8.7 %all_to_all.70 = bf16[16,2,512]{2,1,0:T(2,128)(2,1)S(1)} all-to-all(bf16[16,2,512]{2,1,0:T(2,128)(2,1)S(1)} %reshape.219), channel_id=1, replica_groups=mesh['seq'=8,'head'=16] {'head'}, dimensions={0} | all-to-all | bytes 65536 | tf_op jit(solution)/shard_map/all_to_all | solution.py:135
  335.3 2.1 fusion.37
  337.5 5.3 %fusion.19 = bf16[1024,1024]{1,0:T(8,128)(2,1)} fusion(f32[1024,1024]{1,0:T(8,128)} %get-tuple-element.141, f32[16,1024]{1,0:T(8,128)S(1)} %fusion.37, bf16[1024,1024]{1,0:T(8,128)(2,1)S(1)} %copy-done.3, pred[1024]{0:T(1024)(128)(4,1)S(1)} %copy-done.12, bf16[1024]{0:T(1024)(128)(2,1)S(1)} %copy-done.16, pred[1024]{0:T(1024)(128)(4,1)S(1)} %copy-done.14), kind=kLoop, calls=%fused_computation.36 | loop fusion | flops 8388608 | bytes 8458240 | tf_op jit(solution)/shard_map/convert_element_type | solution.py:137
  (75 shorter events, 3.7 us)
Async XLA Ops:
  0.0 175.7 %copy-start = (bf16[1024,1024]{1,0:T(8,128)(2,1)S(1)}, bf16[1024,1024]{1,0:T(8,128)(2,1)}, u32[]{:S(2)}) copy-start(bf16[1024,1024]{1,0:T(8,128)(2,1)} %param.24) | copy-start | bytes 6291460
  1.6 29.1 %copy-start.11 = (pred[1024]{0:T(1024)(128)(4,1)}, pred[1024]{0:T(1024)(128)(4,1)S(1)}, u32[]{:S(2)}) copy-start(pred[1024]{0:T(1024)(128)(4,1)S(1)} %get-tuple-element.144) | copy-start | bytes 3076
  1.6 29.1 %copy-start.13 = (pred[1024]{0:T(1024)(128)(4,1)}, pred[1024]{0:T(1024)(128)(4,1)S(1)}, u32[]{:S(2)}) copy-start(pred[1024]{0:T(1024)(128)(4,1)S(1)} %get-tuple-element.145) | copy-start | bytes 3076
  1.6 7.4 %copy-start.15 = (bf16[1024]{0:T(1024)(128)(2,1)S(1)}, bf16[1024]{0:T(1024)(128)(2,1)}, u32[]{:S(2)}) copy-start(bf16[1024]{0:T(1024)(128)(2,1)} %param.19) | copy-start | bytes 6148
  8.9 2.7 copy-start.17
  8.9 2.7 copy-start.2
  11.7 5.2 %copy-start.19 = (bf16[1024,1024]{1,0:T(8,128)(2,1)S(1)}, bf16[1024,1024]{1,0:T(8,128)(2,1)}, u32[]{:S(2)}) copy-start(bf16[1024,1024]{1,0:T(8,128)(2,1)} %param.22) | copy-start | bytes 6291460
  16.9 3.5 %copy-start.4 = (bf16[1024,1024]{0,1:T(8,128)(2,1)}, bf16[1024,1024]{0,1:T(8,128)(2,1)S(1)}, u32[]{:S(2)}) copy-start(bf16[1024,1024]{0,1:T(8,128)(2,1)S(1)} %convolution_convert_fusion.1) | copy-start | bytes 6291460
  20.4 5.5 %copy-start.6 = (bf16[1024,1024]{0,1:T(8,128)(2,1)}, bf16[1024,1024]{0,1:T(8,128)(2,1)S(1)}, u32[]{:S(2)}) copy-start(bf16[1024,1024]{0,1:T(8,128)(2,1)S(1)} %convolution_convert_fusion.2) | copy-start | bytes 6291460
  20.4 9.6 %copy-start.18 = (bf16[1024]{0:T(1024)(128)(2,1)S(1)}, bf16[1024]{0:T(1024)(128)(2,1)}, u32[]{:S(2)}) copy-start(bf16[1024]{0:T(1024)(128)(2,1)} %param.25) | copy-start | bytes 6148
  25.9 11.0 %collective-permute-start = (bf16[512,2048]{0,1:T(8,128)(2,1)}, bf16[512,2048]{0,1:T(8,128)(2,1)}, u32[]{:S(2)}, u32[]{:S(2)}) collective-permute-start(bf16[512,2048]{0,1:T(8,128)(2,1)} %get-tuple-element.138), channel_id=1, source_target_pairs={{0,1},{1,2},{2,3},{3,4},{4,5},{5,6},{6,7},{7,8},{8,9},{9,10},{10,1... | collective-permute-start | bytes 6291464 | tf_op jit(solution)/shard_map/ppermute | solution.py:16
  28.5 8.3 %collective-permute-start.1 = (bf16[512,2048]{0,1:T(8,128)(2,1)}, bf16[512,2048]{0,1:T(8,128)(2,1)}, u32[]{:S(2)}, u32[]{:S(2)}) collective-permute-start(bf16[512,2048]{0,1:T(8,128)(2,1)} %get-tuple-element.139), channel_id=1, source_target_pairs={{1,0},{2,1},{3,2},{4,3},{5,4},{6,5},{7,6},{8,7},{9,8},{10,9},{11,1... | collective-permute-start | bytes 6291464 | tf_op jit(solution)/shard_map/ppermute | solution.py:19
  30.6 6.2 %copy-start.5 = (bf16[1024,1024]{0,1:T(8,128)(2,1)S(1)}, bf16[1024,1024]{0,1:T(8,128)(2,1)}, u32[]{:S(2)}) copy-start(bf16[1024,1024]{0,1:T(8,128)(2,1)} %copy-done.4) | copy-start | bytes 6291460
  30.6 6.2 %copy-start.7 = (bf16[1024,1024]{0,1:T(8,128)(2,1)S(1)}, bf16[1024,1024]{0,1:T(8,128)(2,1)}, u32[]{:S(2)}) copy-start(bf16[1024,1024]{0,1:T(8,128)(2,1)} %copy-done.6) | copy-start | bytes 6291460
  61.0 114.8 %copy-start.12 = (pred[1024]{0:T(1024)(128)(4,1)S(1)}, pred[1024]{0:T(1024)(128)(4,1)}, u32[]{:S(2)}) copy-start(pred[1024]{0:T(1024)(128)(4,1)} %copy-done.11) | copy-start | bytes 3076
  61.0 114.8 %copy-start.14 = (pred[1024]{0:T(1024)(128)(4,1)S(1)}, pred[1024]{0:T(1024)(128)(4,1)}, u32[]{:S(2)}) copy-start(pred[1024]{0:T(1024)(128)(4,1)} %copy-done.13) | copy-start | bytes 3076
  61.0 114.8 %copy-start.16 = (bf16[1024]{0:T(1024)(128)(2,1)S(1)}, bf16[1024]{0:T(1024)(128)(2,1)}, u32[]{:S(2)}) copy-start(bf16[1024]{0:T(1024)(128)(2,1)} %param.19) | copy-start | bytes 6148
  175.7 7.1 %copy-start.10 = (f32[1024]{0:T(1024)S(1)}, f32[1024]{0:T(1024)}, u32[]{:S(2)}) copy-start(f32[1024]{0:T(1024)} %convert_element_type.93) | copy-start | bytes 12292
  175.8 7.2 %copy-start.8 = (bf16[1024,1024]{1,0:T(8,128)(2,1)S(1)}, bf16[1024,1024]{1,0:T(8,128)(2,1)}, u32[]{:S(2)}) copy-start(bf16[1024,1024]{1,0:T(8,128)(2,1)} %param.27) | copy-start | bytes 6291460
  184.2 52.1 %all-to-all-start.1 = ((bf16[16,2,512]{2,1,0:T(2,128)(2,1)}), bf16[16,2,512]{2,1,0:T(2,128)(2,1)S(1)}, u32[]{:S(2)}, u32[]{:S(2)}) async-start(bf16[16,2,512]{2,1,0:T(2,128)(2,1)} %reshape.217), calls=%async_computation.1 | async-start | bytes 65536 | tf_op jit(solution)/shard_map/all_to_all | solution.py:113
  230.2 2.2 copy-start.9
  236.3 39.1 %all-to-all-start = ((bf16[16,2,512]{2,1,0:T(2,128)(2,1)}), bf16[16,2,512]{2,1,0:T(2,128)(2,1)S(1)}, u32[]{:S(2)}, u32[]{:S(2)}) async-start(bf16[16,2,512]{2,1,0:T(2,128)(2,1)} %reshape.215), calls=%async_computation | async-start | bytes 65536 | tf_op jit(solution)/shard_map/all_to_all | solution.py:112
  275.4 12.1 %all-to-all-start.2 = ((bf16[16,2,512]{2,1,0:T(2,128)(2,1)}), bf16[16,2,512]{2,1,0:T(2,128)(2,1)S(1)}, u32[]{:S(2)}, u32[]{:S(2)}) async-start(bf16[16,2,512]{2,1,0:T(2,128)(2,1)} %reshape.213), calls=%async_computation.2 | async-start | bytes 65536 | tf_op jit(solution)/shard_map/all_to_all | solution.py:114
  287.6 37.0 %copy-start.1 = (f32[256,2048]{1,0:T(8,128)S(1)}, f32[256,2048]{1,0:T(8,128)}, u32[]{:S(2)}) copy-start(f32[256,2048]{1,0:T(8,128)} %get-tuple-element.143) | copy-start | bytes 6291460
  335.3 2.2 copy-start.3
where the time goes:
time: 345 us; the launch traced here: 343 us
  matrix products  116 us (34%)
  blocking collectives  78.7 us (23%)
  starting transfers between devices  60 us (17%)
  other arithmetic  42.2 us (12%)
  local copies, waits for them, and re-layouts  38.1 us (11%)
  waiting for transfers between devices  5.96 us (2%)
    sub x2, matrix products, local_block(): probs = jnp.exp(scores - top)  46.1 us
    all_to_all x1, starting transfers between devices, body(): lax.all_to_all(ck, 'head', split_axis=1, concat_axis=0, tiled=True)  46 us
    dot_general x2, matrix products, local_block(): jnp.einsum('hqk,khd->qhd', probs, vh, preferred_element_type=jnp.float32)  39.6 us
    all_gather x1, blocking collectives, body(): part_k = lax.all_gather(head_k, 'seq', axis=0, tiled=True)  35 us
    all_gather x1, blocking collectives, body(): part_v = lax.all_gather(head_v, 'seq', axis=0, tiled=True)  35 us
    concatenate x1, other arithmetic, with_halo(): block = jnp.concatenate([low, block, high], axis=dim)  20.3 us
    dot_general x6, matrix products, project(): jnp.dot(rows, weight, preferred_element_type=jnp.float32)  17.7 us
    dynamic_slice x2, local copies, waits for them, and re-layouts, one_block(): k_rows = lax.dynamic_slice_in_dim(keys_ext, first, block + 2 * HALF_WIN, 0)  11.7 us
  transfers between devices with their start and end apart: 5, of which 2 were waited for; matrix products, arithmetic and copies ran while one was open for 4% of the time, Pallas kernels for 0%

commit v1 on v0

v1 whole, which is shorter than its diff:
```python
import functools
import math

import jax
import jax.numpy as jnp
from jax import lax
from jax.experimental import pallas as pl
from jax.experimental.pallas import tpu as pltpu
from jax.sharding import Mesh
from jax.sharding import PartitionSpec as P

D = 1024
HEADS = 16
WIDTH = 64
VOCAB = 512
ROWS = VOCAB + 16
HALF_WIN = 512
POOL = 64
TILE = 512
SUB = 256
GROUP = 4
COLS = GROUP * WIDTH
VROWS = WIDTH + 16
MIB = 1 << 20
ALL = ("x_hi", "x_lo", "y_hi", "z_hi", "z_lo", "y_lo", "core")
RING = ("z_hi", "z_lo", "core")
PLANE = ("x_hi", "x_lo", "y_hi", "y_lo")
F32 = jnp.float32
BF16 = jnp.bfloat16


def dot(a, b):
    return jnp.dot(a, b, preferred_element_type=F32)


def dot_nt(a, b):
    return lax.dot_general(a, b, (((1,), (1,)), ((), ())), preferred_element_type=F32)


def dot_tn(a, b):
    return lax.dot_general(a, b, (((0,), (0,)), ((), ())), preferred_element_type=F32)


def normalize(rows, gain):
    wide = rows.astype(F32)
    scaled = wide * lax.rsqrt(jnp.mean(wide * wide, axis=-1, keepdims=True) + 1e-05)
    return (scaled * gain.astype(F32)).astype(BF16)


def rounded(x):
    return x.astype(BF16).astype(F32)


def one_hot(ids):
    event = lax.broadcasted_iota(jnp.int32, (ROWS, ids.shape[1]), 0) + 1
    return jnp.where(event == ids, 1.0, 0.0).astype(BF16)


def local_kernel(
    low, own, high, mask_embed, gain, cgain, embed_hbm, lq, lk, lv, wout_hbm, cq, ck, cv,
    att, payload,
    hot, logs, scores, pooled_in, matt, embed, local_w, weights, normed, k3, vt, att_out,
    sem_e, sem_l, sem_w, sem_o,
):
    step = pl.program_id(0)
    rows = att.shape[0]
    steps = HEADS // GROUP
    embed_copy = pltpu.make_async_copy(embed_hbm, embed, sem_e)

    def local_copy(i, g):
        src = (lq, lk, lv)[i].at[:, pl.ds(pl.multiple_of(g * COLS, COLS), COLS)]
        return pltpu.make_async_copy(src, local_w.at[i, g], sem_l.at[i, g])

    late_copies = [
        pltpu.make_async_copy(src, weights.at[i], sem_w.at[i])
        for i, src in enumerate((wout_hbm, cq, ck, cv))
    ]

    def out_copy(g):
        dst = att.at[:, pl.ds(pl.multiple_of(g * COLS, COLS), COLS)]
        return pltpu.make_async_copy(att_out.at[g], dst, sem_o.at[g])

    @pl.when(step == 0)
    def _():
        embed_copy.start()
        for g in range(steps):
            for i in range(3):
                local_copy(i, g).start()
        for copy in late_copies:
            copy.start()
        hot[:, 0:HALF_WIN] = one_hot(low[...].reshape(1, HALF_WIN))
        hot[:, HALF_WIN : HALF_WIN + rows] = one_hot(own[...].reshape(1, rows))
        hot[:, HALF_WIN + rows :] = one_hot(high[...].reshape(1, HALF_WIN))
        j = lax.broadcasted_iota(jnp.int32, (SUB, SUB), 0)
        i = lax.broadcasted_iota(jnp.int32, (SUB, SUB), 1)
        first = jnp.where(j >= i, 1.0, 0.0).astype(BF16)
        last = jnp.where(j <= i, 1.0, 0.0).astype(BF16)
        every = jnp.ones((SUB, SUB), BF16)
        span = 2 * HALF_WIN // SUB
        for t in range(rows // SUB):
            block = lambda b: hot[:, (t + b) * SUB : (t + b + 1) * SUB]
            inner = block(1)
            for b in range(2, span):
                inner = inner + block(b)
            count = dot(block(0), first) + dot(inner, every) + dot(block(span), last)
            logs[:, t * SUB : (t + 1) * SUB] = jnp.where(
                count > 0.0, jnp.log(jnp.maximum(count, 1.0)) * math.log2(math.e), -1e30
            )
        row = lax.broadcasted_iota(jnp.int32, (16, rows), 0)
        col = lax.broadcasted_iota(jnp.int32, (16, rows), 1)
        member = jnp.where(col // POOL == row, 1.0 / POOL, 0.0).astype(BF16)
        share = dot_nt(member, hot[:, HALF_WIN : HALF_WIN + rows])
        embed_copy.wait()
        mask_row = mask_embed[...].reshape(1, D)
        gain_row = gain[...].reshape(1, D)
        pooled_in[...] = dot(share[:, 0:VOCAB].astype(BF16), embed[...]) + share[
            :, VOCAB : VOCAB + 1
        ] * mask_row.astype(F32)
        normed[0:VOCAB, :] = normalize(embed[...], gain_row)
        keep = lax.broadcasted_iota(jnp.int32, (16, D), 0) == 0
        row = jnp.broadcast_to(normalize(mask_row, gain_row).astype(F32), (16, D))
        normed[VOCAB:ROWS, :] = jnp.where(keep, row, 0.0).astype(BF16)

    for i in range(3):
        local_copy(i, step).wait()
    q = rounded(dot(normed[...], local_w[0, step]))
    qt = q[0:VOCAB].T.astype(BF16)
    qm = jnp.broadcast_to(q[VOCAB : VOCAB + 1], (128, COLS)).T
    k = rounded(dot(normed[...], local_w[1, step])) * (math.log2(math.e) * WIDTH**-0.5)
    k_a = k.astype(BF16)
    rest = k - k_a.astype(F32)
    k_b = rest.astype(BF16)
    k_c = (rest - k_b.astype(F32)).astype(BF16)
    v = rounded(dot(normed[...], local_w[2, step]))
    v_t = v[0:VOCAB].T
    v_m = jnp.broadcast_to(v[VOCAB : VOCAB + 1], (128, COLS)).T
    ones = jnp.where(lax.broadcasted_iota(jnp.int32, (16, VOCAB), 0) == 0, 1.0, 0.0)
    vm = []
    for h in range(GROUP):
        s = slice(h * WIDTH, (h + 1) * WIDTH)
        k3[h] = jnp.concatenate([k_a[:, s], k_b[:, s], k_c[:, s]], axis=1)
        vt[h] = jnp.concatenate([v_t[s], ones], axis=0).astype(BF16)
        vm.append(jnp.concatenate([v_m[s], ones[:, 0:128]], axis=0))

    queries = []
    for t in range(rows // TILE):
        own_cols = slice(HALF_WIN + t * TILE, HALF_WIN + (t + 1) * TILE)
        masked = hot[VOCAB:ROWS, own_cols].astype(F32)[0:1]
        x = dot(qt, hot[0:VOCAB, own_cols])
        x = x + jnp.concatenate([qm] * (TILE // 128), axis=1) * masked
        queries.append(x.astype(BF16))

    units = [(t, h) for t in range(rows // TILE) for h in range(GROUP)]

    def score(u):
        t, h = units[u]
        q_h = queries[t][h * WIDTH : (h + 1) * WIDTH]
        s = dot(k3[h], jnp.concatenate([q_h, q_h, q_h], axis=0))
        s = s + logs[:, t * TILE : (t + 1) * TILE]
        scores[u % 2] = s
        return jnp.max(s, axis=0, keepdims=True)

    def mix(u, top):
        h = units[u][1]
        probs = jnp.exp2((scores[u % 2] - top).astype(BF16))
        mixed = dot(vt[h], probs[0:VOCAB])
        last = probs[VOCAB:ROWS].astype(F32)[0:1]
        mixed = mixed + jnp.concatenate([vm[h]] * (TILE // 128), axis=1) * last
        return mixed[0:WIDTH] * (1.0 / mixed[WIDTH : WIDTH + 1])

    top = score(0)
    held = None
    for u, (t, h) in enumerate(units):
        later = score(u + 1) if u + 1 < len(units) else None
        mixed = mix(u, top)
        top = later
        if h % 2 == 0:
            held = mixed
            continue
        out = jnp.concatenate([held, mixed], axis=0).T
        cols = slice((h - 1) * WIDTH, (h + 1) * WIDTH)
        att_out[step, t * TILE : (t + 1) * TILE, cols] = out.astype(BF16)
        each = TILE // POOL
        mean = jnp.sum(out.reshape(each, POOL, 128), axis=1) * (1.0 / POOL)
        matt[step, t * each : (t + 1) * each, cols] = mean
    out_copy(step).start()

    @pl.when(step == steps - 1)
    def _():
        for copy in late_copies:
            copy.wait()
        mean = jnp.concatenate([matt[g] for g in range(steps)], axis=1)
        head = mean.astype(BF16)
        tail = (mean - head.astype(F32)).astype(BF16)
        lifted = dot(jnp.concatenate([head, tail], axis=0), weights[0])
        pooled = (pooled_in[...] + lifted[0:16] + lifted[16:32]).astype(BF16)
        coarse = normalize(pooled, cgain[...].reshape(1, D))
        q = rounded(dot(coarse, weights[1]))
        k = rounded(dot(coarse, weights[2]))
        v = rounded(dot(coarse, weights[3]))
        for h in range(HEADS):
            s = slice(h * WIDTH, (h + 1) * WIDTH)
            kv = jnp.concatenate([k[:, s], v[:, s]], axis=1)
            qq = jnp.concatenate([q[0:8, s], q[8:16, s]], axis=1)
            payload[h] = jnp.concatenate([kv, qq], axis=0).astype(BF16)
        for g in range(steps):
            out_copy(g).wait()


def local_attention(low, own, high, mask_embed, gain, cgain, *arrays):
    steps = HEADS // GROUP
    rows = own.shape[0]
    whole = lambda shape: pl.BlockSpec(shape, lambda g: (0,) * len(shape))
    hbm = pl.BlockSpec(memory_space=pl.ANY)
    small = (low, own, high, mask_embed, gain, cgain)
    return pl.pallas_call(
        local_kernel,
        grid=(steps,),
        in_specs=[whole(x.shape) for x in small] + [hbm] * len(arrays),
        out_specs=[hbm, whole((HEADS, 24, 128))],
        out_shape=[
            jax.ShapeDtypeStruct((rows, D), BF16),
            jax.ShapeDtypeStruct((HEADS, 24, 128), BF16),
        ],
        scratch_shapes=[
            pltpu.VMEM((ROWS, rows + 2 * HALF_WIN), BF16),
            pltpu.VMEM((ROWS, rows), F32),
            pltpu.VMEM((2, ROWS, TILE), F32),
            pltpu.VMEM((16, D), F32),
            pltpu.VMEM((steps, rows // POOL, COLS), F32),
            pltpu.VMEM((VOCAB, D), BF16),
            pltpu.VMEM((3, steps, D, COLS), BF16),
            pltpu.VMEM((4, D, D), BF16),
            pltpu.VMEM((ROWS, D), BF16),
            pltpu.VMEM((GROUP, ROWS, 3 * WIDTH), BF16),
            pltpu.VMEM((GROUP, VROWS, VOCAB), BF16),
            pltpu.VMEM((steps, rows, COLS), BF16),
            pltpu.SemaphoreType.DMA(()),
            pltpu.SemaphoreType.DMA((3, steps)),
            pltpu.SemaphoreType.DMA((4,)),
            pltpu.SemaphoreType.DMA((steps,)),
        ],
        compiler_params=pltpu.CompilerParams(vmem_limit_bytes=60 * MIB),
        cost_estimate=pl.CostEstimate(
            flops=16 * rows * ROWS * D, bytes_accessed=20 * MIB, transcendentals=rows * ROWS * HEADS
        ),
        name="local",
    )(*small, *arrays)


def mid_kernel(ids, att, embed, mask_embed, wout, mid):
    hot = one_hot(ids[...].reshape(1, SUB))
    total = dot(att[...], wout[...]) + dot_tn(hot[0:VOCAB], embed[...])
    row = jnp.broadcast_to(mask_embed[...].reshape(1, D), (16, D))
    total = total + dot_tn(hot[VOCAB:ROWS], row)
    mid[...] = total.astype(BF16)


def make_mid(ids, att, embed, mask_embed, wout):
    rows = att.shape[0]
    whole = lambda shape: pl.BlockSpec(shape, lambda g: (0,) * len(shape))
    return pl.pallas_call(
        mid_kernel,
        grid=(rows // SUB,),
        in_specs=[
            pl.BlockSpec((SUB,), lambda g: (g,)),
            pl.BlockSpec((SUB, D), lambda g: (g, 0)),
            whole((VOCAB, D)),
            whole((D,)),
            whole((D, D)),
        ],
        out_specs=pl.BlockSpec((SUB, D), lambda g: (g, 0)),
        out_shape=jax.ShapeDtypeStruct((rows, D), BF16),
        compiler_params=pltpu.CompilerParams(vmem_limit_bytes=60 * MIB),
        cost_estimate=pl.CostEstimate(
            flops=2 * rows * (ROWS + D) * D, bytes_accessed=8 * MIB, transcendentals=0
        ),
        name="mid",
    )(ids, att, embed, mask_embed, wout)


def coarse_kernel(q, kv, out):
    x = q[...].astype(F32).reshape(q.shape[0] * 8, 128) * WIDTH**-0.5
    low = lax.broadcasted_iota(jnp.int32, x.shape, 1) < WIDTH
    both = jnp.concatenate(
        [jnp.where(low, x, 0.0), jnp.where(low, pltpu.roll(x, WIDTH, 1), 0.0)], axis=0
    ).astype(BF16)
    scores = dot_nt(both, kv[...])
    probs = jnp.exp(scores - jnp.max(scores, axis=1, keepdims=True))
    total = jnp.sum(probs, axis=1, keepdims=True)
    mixed = dot(probs.astype(BF16), kv[...]) * (1.0 / total)
    half = x.shape[0]
    packed = jnp.where(low, pltpu.roll(mixed[0:half], WIDTH, 1), mixed[half:])
    out[...] = packed.reshape(out.shape).astype(BF16)


def coarse_attention(q, kv):
    vmem = pl.BlockSpec(memory_space=pltpu.VMEM)
    return pl.pallas_call(
        coarse_kernel,
        in_specs=[vmem, vmem],
        out_shape=jax.ShapeDtypeStruct(q.shape, BF16),
        compiler_params=pltpu.CompilerParams(vmem_limit_bytes=32 * MIB),
        cost_estimate=pl.CostEstimate(
            flops=8 * 10**9, bytes_accessed=16 * MIB, transcendentals=1 << 19
        ),
        name="coarse",
    )(q, kv)


def final_kernel(back, wout, mid, out, lifted):
    step = pl.program_id(0)

    @pl.when(step == 0)
    def _():
        low = lax.broadcasted_iota(jnp.int32, (8, 128), 1) < WIDTH
        top, bottom = [], []
        for pair in range(HEADS // 2):
            a = back[2 * pair].astype(F32)
            b = back[2 * pair + 1].astype(F32)
            top.append(jnp.where(low, a, pltpu.roll(b, WIDTH, 1)))
            bottom.append(jnp.where(low, pltpu.roll(a, WIDTH, 1), b))
        rows = [jnp.concatenate(top, axis=1), jnp.concatenate(bottom, axis=1)]
        lifted[...] = dot(jnp.concatenate(rows, axis=0).astype(BF16), wout[...])

    each = mid.shape[0] // POOL
    for r in range(each):
        s = slice(r * POOL, (r + 1) * POOL)
        add = lifted[pl.ds(step * each + r, 1), :]
        out[s, :] = (mid[s, :].astype(F32) + add).astype(BF16)


def finish(back, wout, mid):
    rows = mid.shape[0]
    whole = lambda shape: pl.BlockSpec(shape, lambda g: (0,) * len(shape))
    return pl.pallas_call(
        final_kernel,
        grid=(rows // SUB,),
        in_specs=[
            whole(back.shape),
            whole((D, D)),
            pl.BlockSpec((SUB, D), lambda g: (g, 0)),
        ],
        out_specs=pl.BlockSpec((SUB, D), lambda g: (g, 0)),
        out_shape=jax.ShapeDtypeStruct((rows, D), BF16),
        scratch_shapes=[pltpu.VMEM((16, D), F32)],
        compiler_params=pltpu.CompilerParams(vmem_limit_bytes=20 * MIB),
        name="finish",
    )(back, wout, mid)


def body(
    token_ids,
    bar_mask,
    embed,
    mask_embed,
    local_gain,
    local_query,
    local_key,
    local_value,
    local_out,
    coarse_gain,
    coarse_query,
    coarse_key,
    coarse_value,
    coarse_out,
):
    rows = token_ids.shape[0]
    own = jnp.where(bar_mask == 1, VOCAB + 1, token_ids + 1)
    count = lax.axis_size(ALL)
    forward = [(i, i + 1) for i in range(count - 1)]
    backward = [(b, a) for a, b in forward]
    low = lax.ppermute(own[rows - HALF_WIN :], ALL, forward)
    high = lax.ppermute(own[:HALF_WIN], ALL, backward)
    att, payload = local_attention(
        low, own, high, mask_embed, local_gain, coarse_gain, embed,
        local_query, local_key, local_value, local_out, coarse_query, coarse_key, coarse_value,
    )
    got = lax.all_to_all(payload, PLANE, split_axis=0, concat_axis=0, tiled=True)
    q = got[:, 16:24]
    kv = got[:, 0:16].reshape(1, HEADS * 16, 128)
    peers = lax.axis_size(RING)
    kv = jnp.broadcast_to(kv, (peers,) + kv.shape[1:])
    kv = lax.all_to_all(kv, RING, split_axis=0, concat_axis=0, tiled=True)
    mid = make_mid(own, att, embed, mask_embed, local_out)
    kv, mid = lax.optimization_barrier((kv, mid))
    mixed = coarse_attention(q, kv.reshape(peers * HEADS * 16, 128))
    back = lax.all_to_all(mixed, PLANE, split_axis=0, concat_axis=0, tiled=True)
    return finish(back, coarse_out, mid)


def solution(mesh):
    fine = Mesh(mesh.devices.reshape((2,) * len(ALL)), ALL)
    placed = (P(ALL),) * 2 + (P(),) * 12
    return jax.shard_map(
        body, mesh=fine, in_specs=placed, out_specs=P(ALL, None), check_vma=False
    )
```

time: 345 us -> 79.6 us (0.23)
  matrix products: 116 us -> 0 us
  starting transfers between devices: 60 us -> 7.72 us
  blocking collectives: 78.7 us -> 28.8 us
  other arithmetic: 42.2 us -> 0.71 us
  local copies, waits for them, and re-layouts: 38.1 us -> 1.49 us
  Pallas kernels: 0 us -> 34.1 us
    all_gather x2 -> x0, blocking collectives: 70 us -> none  [the longest x1 35 us: body(): part_k = lax.all_gather(head_k, 'seq', axis=0, tiled=True)]
    dot_general x12 -> x0, matrix products: 69.7 us -> none  [the longest x2 39.6 us: local_block(): jnp.einsum('hqk,khd->qhd', probs, vh, preferred_element_type=jnp.float32)]
    all_to_all x3 -> x1, starting transfers between devices: 55.9 us -> 5.14 us  [body(): kv = lax.all_to_all(kv, RING, split_axis=0, concat_axis=0, tiled=True)]
    sub x2 -> x0, matrix products: 46.1 us -> none  [local_block(): probs = jnp.exp(scores - top)]
    pallas_call x0 -> x4, Pallas kernels: none -> 34.1 us  [the longest x1 23 us: local_attention(): pl.pallas_call(local_kernel, grid=(steps,), in_specs=[whole(x.shape) for...]
    concatenate x2 -> x0, other arithmetic: 25.8 us -> none  [the longest x1 20.3 us: with_halo(): block = jnp.concatenate([low, block, high], axis=dim)]
    all_to_all x1 -> x2, blocking collectives: 8.67 us -> 28.8 us  [the longest x1 17.7 us: body(): lax.all_to_all(payload, PLANE, split_axis=0, concat_axis=0, tiled=True)]
    dynamic_slice x8 -> x0, local copies, waits for them, and re-layouts: 18.2 us -> none  [the longest x2 11.7 us: one_block(): k_rows = lax.dynamic_slice_in_dim(keys_ext, first, block + 2 * HALF_WIN, 0)]
  transfers between devices with their start and end apart: 5 -> 3, of which waited for: 2 -> 2; matrix products, arithmetic and copies ran while one was open for 4% -> 0% of each run, Pallas kernels for 0% -> 10%
where the time goes in v1:
time: 79.6 us; the launch traced here: 79.1 us
  Pallas kernels  34.1 us (43%)
  blocking collectives  28.8 us (36%)
  starting transfers between devices  7.72 us (10%)
  waiting for transfers between devices  6.33 us (8%)
  local copies, waits for them, and re-layouts  1.49 us (2%)
    pallas_call x1, Pallas kernels, local_attention(): pl.pallas_call(local_kernel, grid=(steps,), in_specs=[whole(x.shape) for...  23 us
    all_to_all x1, blocking collectives, body(): lax.all_to_all(payload, PLANE, split_axis=0, concat_axis=0, tiled=True)  17.7 us
    all_to_all x1, blocking collectives, body(): back = lax.all_to_all(mixed, PLANE, split_axis=0, concat_axis=0, tiled=True)  11.1 us
    pallas_call x1, Pallas kernels, make_mid(): pl.pallas_call(mid_kernel, grid=(rows // SUB,), in_specs=[pl.BlockSpec((S...  7.64 us
    all_to_all x1, starting transfers between devices, body(): kv = lax.all_to_all(kv, RING, split_axis=0, concat_axis=0, tiled=True)  5.14 us
    ppermute x1, waiting for transfers between devices, body(): high = lax.ppermute(own[:HALF_WIN], ALL, backward)  3.63 us
    all_to_all x1, waiting for transfers between devices, body(): kv = lax.all_to_all(kv, RING, split_axis=0, concat_axis=0, tiled=True)  2.71 us
    pallas_call x1, Pallas kernels, finish(): pl.pallas_call(final_kernel, grid=(rows // SUB,), in_specs=[whole(back.sh...  2.37 us
  transfers between devices with their start and end apart: 3, of which 2 were waited for; matrix products, arithmetic and copies ran while one was open for 0% of the time, Pallas kernels for 10%

profile of v1, /device:TPU:0, one launch (start us, length us, event | category | flops | bytes accessed | tf_op | source)
XLA Modules:
  0.0 79.1 jit_solution(9556381944184650273)
XLA Ops:
  0.0 0.7 add_select_fusion.own.ids
  0.7 0.0 copy-start.2
  0.7 1.3 %collective-permute-start = (s32[512]{0:T(512)S(1)}, s32[512]{0:T(512)S(1)}, u32[]{:S(2)}, u32[]{:S(2)}) collective-permute-start(s32[512]{0:T(512)S(1)} %get-tuple-element.14), channel_id=1, source_target_pairs={{0,1},{1,2},{2,3},{3,4},{4,5},{5,6},{6,7},{7,8},{8,9},{9,10},{10,1... | collective-permute-start | bytes 6152 | tf_op jit(solution)/shard_map/ppermute | solution.py:373
  2.0 1.3 %collective-permute-start.1 = (s32[512]{0:T(512)S(1)}, s32[512]{0:T(512)S(1)}, u32[]{:S(2)}, u32[]{:S(2)}) collective-permute-start(s32[512]{0:T(512)S(1)} %get-tuple-element.13), channel_id=1, source_target_pairs={{1,0},{2,1},{3,2},{4,3},{5,4},{6,5},{7,6},{8,7},{9,8},{10,9},{11,1... | collective-permute-start | bytes 6152 | tf_op jit(solution)/shard_map/ppermute | solution.py:374
  3.3 0.0 collective-permute-done.low
  3.3 0.0 copy-start.3
  3.3 3.6 %collective-permute-done.1.high = s32[512]{0:T(512)S(1)} collective-permute-done((s32[512]{0:T(512)S(1)}, s32[512]{0:T(512)S(1)}, u32[]{:S(2)}, u32[]{:S(2)}) %collective-permute-start.1) | collective-permute-done | bytes 2080 | tf_op jit(solution)/shard_map/ppermute | solution.py:374
  7.0 0.0 copy-done.2
  7.0 0.0 copy-done.3
  7.0 0.0 copy-start.4
  7.0 0.6 copy-done.4
  7.6 23.0 %local.1 = (bf16[1024,1024]{1,0:T(8,128)(2,1)}, bf16[16,24,128]{2,1,0:T(8,128)(2,1)}) custom-call(s32[512]{0:T(512)} %copy-done.3, s32[1024]{0:T(1024)} %copy-done.2, s32[512]{0:T(512)} %copy-done.4, bf16[1024]{0:T(1024)(128)(2,1)} %mask_embed.3, bf16[1024]{0:T(1024)(128)(2,1)} %gain.1, bf16[1024]{0:T(1024)(128)(2,1)} %cgain.1, bf16[512,1024]{1,0:T(8,128)(2,1)} %embed.1, ...), custom_call_target="tpu_custom_call" | custom-call | flops 8858370048 | bytes 20971520 | tf_op jit(solution)/shard_map/local/pallas_call | solution.py:216
  30.5 17.7 %all_to_all.15 = bf16[16,24,128]{2,1,0:T(8,128)(2,1)S(1)} all-to-all(bf16[16,24,128]{2,1,0:T(8,128)(2,1)} %get-tuple-element.9), channel_id=1, replica_groups=mesh['x_hi'=2,'x_lo'=2,'y_hi'=2,'z_hi'=2,'z_lo'=2,'y_lo'=2,'core'=2] {'x..., dimensions={0} | all-to-all | bytes 196608 | tf_op jit(solution)/shard_map/all_to_all | solution.py:379
  48.2 0.9 %broadcast_in_dim.13 = bf16[8,256,128]{2,1,0:T(8,128)(2,1)} broadcast(bf16[256,128]{1,0:T(8,128)(2,1)S(1)} %bitcast.3), dimensions={1,2} | broadcast | bytes 589824 | tf_op jit(solution)/shard_map/broadcast_in_dim | solution.py:383
  49.1 5.1 %all-to-all-start.1 = ((bf16[8,256,128]{2,1,0:T(8,128)(2,1)}), bf16[8,256,128]{2,1,0:T(8,128)(2,1)S(1)}, u32[]{:S(2)}, u32[]{:S(2)}) async-start(bf16[8,256,128]{2,1,0:T(8,128)(2,1)} %broadcast_in_dim.13), calls=%async_computation.1 | async-start | bytes 1048576 | tf_op jit(solution)/shard_map/all_to_all | solution.py:384
  54.2 7.6 %mid.1 = bf16[1024,1024]{1,0:T(8,128)(2,1)} custom-call(s32[1024]{0:T(1024)} %copy-done.2, bf16[1024,1024]{1,0:T(8,128)(2,1)} %get-tuple-element.10.att, bf16[512,1024]{1,0:T(8,128)(2,1)} %embed.1, bf16[1024]{0:T(1024)(128)(2,1)} %mask_embed.3, bf16[1024,1024]{1,0:T(8,128)(2,1)} %wout.2), custom_call_target="tpu_custom_call" | custom-call | flops 3254779904 | bytes 8388608 | tf_op jit(solution)/shard_map/mid/pallas_call | solution.py:262
  61.9 2.7 %all-to-all-done.1 = bf16[8,256,128]{2,1,0:T(8,128)(2,1)S(1)} async-done(((bf16[8,256,128]{2,1,0:T(8,128)(2,1)}), bf16[8,256,128]{2,1,0:T(8,128)(2,1)S(1)}, u32[]{:S(2)}, u32[]{:S(2)}) %all-to-all-start.1) | async-done | bytes 524320 | tf_op jit(solution)/shard_map/all_to_all | solution.py:384
  64.6 0.0 copy-start
  64.6 0.0 copy-start.1
  64.6 1.1 %coarse.1 = bf16[16,8,128]{2,1,0:T(8,128)(2,1)S(1)} custom-call(bf16[16,8,128]{2,1,0:T(8,128)(2,1)S(1)} %slice.16.q, bf16[2048,128]{1,0:T(8,128)(2,1)S(1)} %bitcast.2), custom_call_target="tpu_custom_call" | custom-call | flops 8000000000 | bytes 16777216 | tf_op jit(solution)/shard_map/coarse/pallas_call | solution.py:299
  65.7 11.1 %all_to_all.16.back = bf16[16,8,128]{2,1,0:T(8,128)(2,1)S(1)} all-to-all(bf16[16,8,128]{2,1,0:T(8,128)(2,1)S(1)} %coarse.1), channel_id=1, replica_groups=mesh['x_hi'=2,'x_lo'=2,'y_hi'=2,'z_hi'=2,'z_lo'=2,'y_lo'=2,'core'=2] {'x..., dimensions={0} | all-to-all | bytes 65536 | tf_op jit(solution)/shard_map/all_to_all | solution.py:388
  76.8 0.0 copy-done
  76.8 0.0 copy-done.1
  76.8 2.4 %finish.1 = bf16[1024,1024]{1,0:T(8,128)(2,1)} custom-call(bf16[16,8,128]{2,1,0:T(8,128)(2,1)S(1)} %all_to_all.16.back, bf16[1024,1024]{1,0:T(8,128)(2,1)S(1)} %copy-done, bf16[1024,1024]{1,0:T(8,128)(2,1)S(1)} %copy-done.1), custom_call_target="tpu_custom_call" | custom-call | tf_op jit(solution)/shard_map/finish/pallas_call | solution.py:336
  (3 shorter events, 0.0 us)
Async XLA Ops:
  0.7 6.2 %copy-start.2 = (s32[1024]{0:T(1024)}, s32[1024]{0:T(1024)S(1)}, u32[]{:S(2)}) copy-start(s32[1024]{0:T(1024)S(1)} %add_select_fusion.own.ids) | copy-start | bytes 12292
  0.7 2.6 %collective-permute-start = (s32[512]{0:T(512)S(1)}, s32[512]{0:T(512)S(1)}, u32[]{:S(2)}, u32[]{:S(2)}) collective-permute-start(s32[512]{0:T(512)S(1)} %get-tuple-element.14), channel_id=1, source_target_pairs={{0,1},{1,2},{2,3},{3,4},{4,5},{5,6},{6,7},{7,8},{8,9},{9,10},{10,1... | collective-permute-start | bytes 6152 | tf_op jit(solution)/shard_map/ppermute | solution.py:373
  2.0 4.9 %collective-permute-start.1 = (s32[512]{0:T(512)S(1)}, s32[512]{0:T(512)S(1)}, u32[]{:S(2)}, u32[]{:S(2)}) collective-permute-start(s32[512]{0:T(512)S(1)} %get-tuple-element.13), channel_id=1, source_target_pairs={{1,0},{2,1},{3,2},{4,3},{5,4},{6,5},{7,6},{8,7},{9,8},{10,9},{11,1... | collective-permute-start | bytes 6152 | tf_op jit(solution)/shard_map/ppermute | solution.py:374
  3.3 3.6 %copy-start.3 = (s32[512]{0:T(512)}, s32[512]{0:T(512)S(1)}, u32[]{:S(2)}) copy-start(s32[512]{0:T(512)S(1)} %collective-permute-done.low) | copy-start | bytes 6148
  7.0 0.6 copy-start.4
  49.1 15.5 %all-to-all-start.1 = ((bf16[8,256,128]{2,1,0:T(8,128)(2,1)}), bf16[8,256,128]{2,1,0:T(8,128)(2,1)S(1)}, u32[]{:S(2)}, u32[]{:S(2)}) async-start(bf16[8,256,128]{2,1,0:T(8,128)(2,1)} %broadcast_in_dim.13), calls=%async_computation.1 | async-start | bytes 1048576 | tf_op jit(solution)/shard_map/all_to_all | solution.py:384
  64.6 12.2 %copy-start = (bf16[1024,1024]{1,0:T(8,128)(2,1)S(1)}, bf16[1024,1024]{1,0:T(8,128)(2,1)}, u32[]{:S(2)}) copy-start(bf16[1024,1024]{1,0:T(8,128)(2,1)} %wout.3) | copy-start | bytes 6291460
  64.6 12.2 %copy-start.1 = (bf16[1024,1024]{1,0:T(8,128)(2,1)S(1)}, bf16[1024,1024]{1,0:T(8,128)(2,1)}, u32[]{:S(2)}) copy-start(bf16[1024,1024]{1,0:T(8,128)(2,1)} %mid.1) | copy-start | bytes 6291460

commit v2 on v1

--- a/solution.py
+++ b/solution.py
@@ -18,6 +18,7 @@
 POOL = 64
 TILE = 512
 SUB = 256
+CHUNK = 48
 GROUP = 4
 COLS = GROUP * WIDTH
 VROWS = WIDTH + 16
@@ -51,6 +52,17 @@
     return x.astype(BF16).astype(F32)
 
 
+def chunks(rows):
+    return [slice(c, min(c + CHUNK, rows)) for c in range(0, rows, CHUNK)]
+
+
+def fill_one_hot(out, first, ids):
+    count = ids.shape[1]
+    for s in chunks(ROWS):
+        event = lax.broadcasted_iota(jnp.int32, (s.stop - s.start, count), 0) + (s.start + 1)
+        out[s, first : first + count] = jnp.where(event == ids, 1.0, 0.0).astype(BF16)
+
+
 def one_hot(ids):
     event = lax.broadcasted_iota(jnp.int32, (ROWS, ids.shape[1]), 0) + 1
     return jnp.where(event == ids, 1.0, 0.0).astype(BF16)
@@ -59,7 +71,7 @@
 def local_kernel(
     low, own, high, mask_embed, gain, cgain, embed_hbm, lq, lk, lv, wout_hbm, cq, ck, cv,
     att, payload,
-    hot, logs, scores, pooled_in, matt, embed, local_w, weights, normed, k3, vt, att_out,
+    hot, logs, scores, probs, pooled_in, matt, embed, local_w, weights, normed, k3, vt, att_out,
     sem_e, sem_l, sem_w, sem_o,
 ):
     step = pl.program_id(0)
@@ -88,9 +100,11 @@
                 local_copy(i, g).start()
         for copy in late_copies:
             copy.start()
-        hot[:, 0:HALF_WIN] = one_hot(low[...].reshape(1, HALF_WIN))
-        hot[:, HALF_WIN : HALF_WIN + rows] = one_hot(own[...].reshape(1, rows))
-        hot[:, HALF_WIN + rows :] = one_hot(high[...].reshape(1, HALF_WIN))
+        fill_one_hot(hot, 0, low[...].reshape(1, HALF_WIN))
+        for c in range(0, rows, HALF_WIN):
+            part = own[c : c + HALF_WIN].reshape(1, HALF_WIN)
+            fill_one_hot(hot, HALF_WIN + c, part)
+        fill_one_hot(hot, HALF_WIN + rows, high[...].reshape(1, HALF_WIN))
         j = lax.broadcasted_iota(jnp.int32, (SUB, SUB), 0)
         i = lax.broadcasted_iota(jnp.int32, (SUB, SUB), 1)
         first = jnp.where(j >= i, 1.0, 0.0).astype(BF16)
@@ -103,9 +117,11 @@
             for b in range(2, span):
                 inner = inner + block(b)
             count = dot(block(0), first) + dot(inner, every) + dot(block(span), last)
-            logs[:, t * SUB : (t + 1) * SUB] = jnp.where(
-                count > 0.0, jnp.log(jnp.maximum(count, 1.0)) * math.log2(math.e), -1e30
-            )
+            for s in chunks(ROWS):
+                c = count[s]
+                logs[s, t * SUB : (t + 1) * SUB] = jnp.where(
+                    c > 0.0, jnp.log(jnp.maximum(c, 1.0)) * math.log2(math.e), -1e30
+                )
         row = lax.broadcasted_iota(jnp.int32, (16, rows), 0)
         col = lax.broadcasted_iota(jnp.int32, (16, rows), 1)
         member = jnp.where(col // POOL == row, 1.0 / POOL, 0.0).astype(BF16)
@@ -116,7 +132,8 @@
         pooled_in[...] = dot(share[:, 0:VOCAB].astype(BF16), embed[...]) + share[
             :, VOCAB : VOCAB + 1
         ] * mask_row.astype(F32)
-        normed[0:VOCAB, :] = normalize(embed[...], gain_row)
+        for c in range(0, VOCAB, 32):
+            normed[c : c + 32, :] = normalize(embed[c : c + 32], gain_row)
         keep = lax.broadcasted_iota(jnp.int32, (16, D), 0) == 0
         row = jnp.broadcast_to(normalize(mask_row, gain_row).astype(F32), (16, D))
         normed[VOCAB:ROWS, :] = jnp.where(keep, row, 0.0).astype(BF16)
@@ -126,11 +143,16 @@
     q = rounded(dot(normed[...], local_w[0, step]))
     qt = q[0:VOCAB].T.astype(BF16)
     qm = jnp.broadcast_to(q[VOCAB : VOCAB + 1], (128, COLS)).T
-    k = rounded(dot(normed[...], local_w[1, step])) * (math.log2(math.e) * WIDTH**-0.5)
-    k_a = k.astype(BF16)
-    rest = k - k_a.astype(F32)
-    k_b = rest.astype(BF16)
-    k_c = (rest - k_b.astype(F32)).astype(BF16)
+    k_all = dot(normed[...], local_w[1, step])
+    for c in chunks(ROWS):
+        k = rounded(k_all[c]) * (math.log2(math.e) * WIDTH**-0.5)
+        k_a = k.astype(BF16)
+        rest = k - k_a.astype(F32)
+        k_b = rest.astype(BF16)
+        k_c = (rest - k_b.astype(F32)).astype(BF16)
+        for h in range(GROUP):
+            s = slice(h * WIDTH, (h + 1) * WIDTH)
+            k3[h, c] = jnp.concatenate([k_a[:, s], k_b[:, s], k_c[:, s]], axis=1)
     v = rounded(dot(normed[...], local_w[2, step]))
     v_t = v[0:VOCAB].T
     v_m = jnp.broadcast_to(v[VOCAB : VOCAB + 1], (128, COLS)).T
@@ -138,7 +160,6 @@
     vm = []
     for h in range(GROUP):
         s = slice(h * WIDTH, (h + 1) * WIDTH)
-        k3[h] = jnp.concatenate([k_a[:, s], k_b[:, s], k_c[:, s]], axis=1)
         vt[h] = jnp.concatenate([v_t[s], ones], axis=0).astype(BF16)
         vm.append(jnp.concatenate([v_m[s], ones[:, 0:128]], axis=0))
 
@@ -156,15 +177,20 @@
         t, h = units[u]
         q_h = queries[t][h * WIDTH : (h + 1) * WIDTH]
         s = dot(k3[h], jnp.concatenate([q_h, q_h, q_h], axis=0))
-        s = s + logs[:, t * TILE : (t + 1) * TILE]
-        scores[u % 2] = s
-        return jnp.max(s, axis=0, keepdims=True)
+        top = None
+        for c in chunks(ROWS):
+            part = s[c] + logs[c, t * TILE : (t + 1) * TILE]
+            scores[u % 2, c] = part
+            peak = jnp.max(part.reshape((c.stop - c.start) // 8, 8, TILE), axis=0)
+            top = peak if top is None else jnp.maximum(top, peak)
+        return jnp.max(top, axis=0, keepdims=True)
 
     def mix(u, top):
         h = units[u][1]
-        probs = jnp.exp2((scores[u % 2] - top).astype(BF16))
-        mixed = dot(vt[h], probs[0:VOCAB])
-        last = probs[VOCAB:ROWS].astype(F32)[0:1]
+        for c in chunks(ROWS):
+            probs[u % 2, c] = jnp.exp2((scores[u % 2, c] - top).astype(BF16))
+        mixed = dot(vt[h], probs[u % 2, 0:VOCAB])
+        last = probs[u % 2, VOCAB:ROWS].astype(F32)[0:1]
         mixed = mixed + jnp.concatenate([vm[h]] * (TILE // 128), axis=1) * last
         return mixed[0:WIDTH] * (1.0 / mixed[WIDTH : WIDTH + 1])
 
@@ -226,6 +252,7 @@
             pltpu.VMEM((ROWS, rows + 2 * HALF_WIN), BF16),
             pltpu.VMEM((ROWS, rows), F32),
             pltpu.VMEM((2, ROWS, TILE), F32),
+            pltpu.VMEM((2, ROWS, TILE), BF16),
             pltpu.VMEM((16, D), F32),
             pltpu.VMEM((steps, rows // POOL, COLS), F32),
             pltpu.VMEM((VOCAB, D), BF16),

time: 79.6 us -> 79.8 us (level)
  no operation moved by 1% of the time
where the time goes in v2:
time: 79.8 us; the launch traced here: 79.4 us
  Pallas kernels  34.3 us (43%)
  blocking collectives  28.8 us (36%)
  starting transfers between devices  7.72 us (10%)
  waiting for transfers between devices  6.33 us (8%)
  local copies, waits for them, and re-layouts  1.49 us (2%)
    pallas_call x1, Pallas kernels, local_attention(): pl.pallas_call(local_kernel, grid=(steps,), in_specs=[whole(x.shape) for...  23.2 us
    all_to_all x1, blocking collectives, body(): lax.all_to_all(payload, PLANE, split_axis=0, concat_axis=0, tiled=True)  17.7 us
    all_to_all x1, blocking collectives, body(): back = lax.all_to_all(mixed, PLANE, split_axis=0, concat_axis=0, tiled=True)  11.1 us
    pallas_call x1, Pallas kernels, make_mid(): pl.pallas_call(mid_kernel, grid=(rows // SUB,), in_specs=[pl.BlockSpec((S...  7.64 us
    all_to_all x1, starting transfers between devices, body(): kv = lax.all_to_all(kv, RING, split_axis=0, concat_axis=0, tiled=True)  5.14 us
    ppermute x1, waiting for transfers between devices, body(): high = lax.ppermute(own[:HALF_WIN], ALL, backward)  3.63 us
    all_to_all x1, waiting for transfers between devices, body(): kv = lax.all_to_all(kv, RING, split_axis=0, concat_axis=0, tiled=True)  2.71 us
    pallas_call x1, Pallas kernels, finish(): pl.pallas_call(final_kernel, grid=(rows // SUB,), in_specs=[whole(back.sh...  2.37 us
  transfers between devices with their start and end apart: 3, of which 2 were waited for; matrix products, arithmetic and copies ran while one was open for 0% of the time, Pallas kernels for 10%

profile of v2, /device:TPU:0, one launch (start us, length us, event | category | flops | bytes accessed | tf_op | source)
XLA Modules:
  0.0 79.4 jit_solution(9041816662625443189)
XLA Ops:
  0.0 0.7 add_select_fusion.own.ids
  0.7 0.0 copy-start.2
  0.7 1.3 %collective-permute-start = (s32[512]{0:T(512)S(1)}, s32[512]{0:T(512)S(1)}, u32[]{:S(2)}, u32[]{:S(2)}) collective-permute-start(s32[512]{0:T(512)S(1)} %get-tuple-element.14), channel_id=1, source_target_pairs={{0,1},{1,2},{2,3},{3,4},{4,5},{5,6},{6,7},{7,8},{8,9},{9,10},{10,1... | collective-permute-start | bytes 6152 | tf_op jit(solution)/shard_map/ppermute | solution.py:400
  2.0 1.3 %collective-permute-start.1 = (s32[512]{0:T(512)S(1)}, s32[512]{0:T(512)S(1)}, u32[]{:S(2)}, u32[]{:S(2)}) collective-permute-start(s32[512]{0:T(512)S(1)} %get-tuple-element.13), channel_id=1, source_target_pairs={{1,0},{2,1},{3,2},{4,3},{5,4},{6,5},{7,6},{8,7},{9,8},{10,9},{11,1... | collective-permute-start | bytes 6152 | tf_op jit(solution)/shard_map/ppermute | solution.py:401
  3.3 0.0 collective-permute-done.low
  3.3 0.0 copy-start.3
  3.3 3.6 %collective-permute-done.1.high = s32[512]{0:T(512)S(1)} collective-permute-done((s32[512]{0:T(512)S(1)}, s32[512]{0:T(512)S(1)}, u32[]{:S(2)}, u32[]{:S(2)}) %collective-permute-start.1) | collective-permute-done | bytes 2080 | tf_op jit(solution)/shard_map/ppermute | solution.py:401
  7.0 0.0 copy-done.2
  7.0 0.0 copy-done.3
  7.0 0.0 copy-start.4
  7.0 0.6 copy-done.4
  7.6 23.2 %local.1 = (bf16[1024,1024]{1,0:T(8,128)(2,1)}, bf16[16,24,128]{2,1,0:T(8,128)(2,1)}) custom-call(s32[512]{0:T(512)} %copy-done.3, s32[1024]{0:T(1024)} %copy-done.2, s32[512]{0:T(512)} %copy-done.4, bf16[1024]{0:T(1024)(128)(2,1)} %mask_embed.3, bf16[1024]{0:T(1024)(128)(2,1)} %gain.1, bf16[1024]{0:T(1024)(128)(2,1)} %cgain.1, bf16[512,1024]{1,0:T(8,128)(2,1)} %embed.1, ...), custom_call_target="tpu_custom_call" | custom-call | flops 8858370048 | bytes 20971520 | tf_op jit(solution)/shard_map/local/pallas_call | solution.py:242
  30.8 17.7 %all_to_all.15 = bf16[16,24,128]{2,1,0:T(8,128)(2,1)S(1)} all-to-all(bf16[16,24,128]{2,1,0:T(8,128)(2,1)} %get-tuple-element.9), channel_id=1, replica_groups=mesh['x_hi'=2,'x_lo'=2,'y_hi'=2,'z_hi'=2,'z_lo'=2,'y_lo'=2,'core'=2] {'x..., dimensions={0} | all-to-all | bytes 196608 | tf_op jit(solution)/shard_map/all_to_all | solution.py:406
  48.5 0.9 %broadcast_in_dim.13 = bf16[8,256,128]{2,1,0:T(8,128)(2,1)} broadcast(bf16[256,128]{1,0:T(8,128)(2,1)S(1)} %bitcast.3), dimensions={1,2} | broadcast | bytes 589824 | tf_op jit(solution)/shard_map/broadcast_in_dim | solution.py:410
  49.3 5.1 %all-to-all-start.1 = ((bf16[8,256,128]{2,1,0:T(8,128)(2,1)}), bf16[8,256,128]{2,1,0:T(8,128)(2,1)S(1)}, u32[]{:S(2)}, u32[]{:S(2)}) async-start(bf16[8,256,128]{2,1,0:T(8,128)(2,1)} %broadcast_in_dim.13), calls=%async_computation.1 | async-start | bytes 1048576 | tf_op jit(solution)/shard_map/all_to_all | solution.py:411
  54.5 7.6 %mid.1 = bf16[1024,1024]{1,0:T(8,128)(2,1)} custom-call(s32[1024]{0:T(1024)} %copy-done.2, bf16[1024,1024]{1,0:T(8,128)(2,1)} %get-tuple-element.10.att, bf16[512,1024]{1,0:T(8,128)(2,1)} %embed.1, bf16[1024]{0:T(1024)(128)(2,1)} %mask_embed.3, bf16[1024,1024]{1,0:T(8,128)(2,1)} %wout.2), custom_call_target="tpu_custom_call" | custom-call | flops 3254779904 | bytes 8388608 | tf_op jit(solution)/shard_map/mid/pallas_call | solution.py:289
  62.1 2.7 %all-to-all-done.1 = bf16[8,256,128]{2,1,0:T(8,128)(2,1)S(1)} async-done(((bf16[8,256,128]{2,1,0:T(8,128)(2,1)}), bf16[8,256,128]{2,1,0:T(8,128)(2,1)S(1)}, u32[]{:S(2)}, u32[]{:S(2)}) %all-to-all-start.1) | async-done | bytes 524320 | tf_op jit(solution)/shard_map/all_to_all | solution.py:411
  64.8 0.0 copy-start
  64.8 0.0 copy-start.1
  64.8 1.1 %coarse.1 = bf16[16,8,128]{2,1,0:T(8,128)(2,1)S(1)} custom-call(bf16[16,8,128]{2,1,0:T(8,128)(2,1)S(1)} %slice.16.q, bf16[2048,128]{1,0:T(8,128)(2,1)S(1)} %bitcast.2), custom_call_target="tpu_custom_call" | custom-call | flops 8000000000 | bytes 16777216 | tf_op jit(solution)/shard_map/coarse/pallas_call | solution.py:326
  65.9 11.1 %all_to_all.16.back = bf16[16,8,128]{2,1,0:T(8,128)(2,1)S(1)} all-to-all(bf16[16,8,128]{2,1,0:T(8,128)(2,1)S(1)} %coarse.1), channel_id=1, replica_groups=mesh['x_hi'=2,'x_lo'=2,'y_hi'=2,'z_hi'=2,'z_lo'=2,'y_lo'=2,'core'=2] {'x..., dimensions={0} | all-to-all | bytes 65536 | tf_op jit(solution)/shard_map/all_to_all | solution.py:415
  77.0 0.0 copy-done
  77.0 0.0 copy-done.1
  77.0 2.4 %finish.1 = bf16[1024,1024]{1,0:T(8,128)(2,1)} custom-call(bf16[16,8,128]{2,1,0:T(8,128)(2,1)S(1)} %all_to_all.16.back, bf16[1024,1024]{1,0:T(8,128)(2,1)S(1)} %copy-done, bf16[1024,1024]{1,0:T(8,128)(2,1)S(1)} %copy-done.1), custom_call_target="tpu_custom_call" | custom-call | tf_op jit(solution)/shard_map/finish/pallas_call | solution.py:363
  (3 shorter events, 0.0 us)
Async XLA Ops:
  0.7 6.2 %copy-start.2 = (s32[1024]{0:T(1024)}, s32[1024]{0:T(1024)S(1)}, u32[]{:S(2)}) copy-start(s32[1024]{0:T(1024)S(1)} %add_select_fusion.own.ids) | copy-start | bytes 12292
  0.7 2.6 %collective-permute-start = (s32[512]{0:T(512)S(1)}, s32[512]{0:T(512)S(1)}, u32[]{:S(2)}, u32[]{:S(2)}) collective-permute-start(s32[512]{0:T(512)S(1)} %get-tuple-element.14), channel_id=1, source_target_pairs={{0,1},{1,2},{2,3},{3,4},{4,5},{5,6},{6,7},{7,8},{8,9},{9,10},{10,1... | collective-permute-start | bytes 6152 | tf_op jit(solution)/shard_map/ppermute | solution.py:400
  2.0 4.9 %collective-permute-start.1 = (s32[512]{0:T(512)S(1)}, s32[512]{0:T(512)S(1)}, u32[]{:S(2)}, u32[]{:S(2)}) collective-permute-start(s32[512]{0:T(512)S(1)} %get-tuple-element.13), channel_id=1, source_target_pairs={{1,0},{2,1},{3,2},{4,3},{5,4},{6,5},{7,6},{8,7},{9,8},{10,9},{11,1... | collective-permute-start | bytes 6152 | tf_op jit(solution)/shard_map/ppermute | solution.py:401
  3.3 3.6 %copy-start.3 = (s32[512]{0:T(512)}, s32[512]{0:T(512)S(1)}, u32[]{:S(2)}) copy-start(s32[512]{0:T(512)S(1)} %collective-permute-done.low) | copy-start | bytes 6148
  7.0 0.6 copy-start.4
  49.3 15.5 %all-to-all-start.1 = ((bf16[8,256,128]{2,1,0:T(8,128)(2,1)}), bf16[8,256,128]{2,1,0:T(8,128)(2,1)S(1)}, u32[]{:S(2)}, u32[]{:S(2)}) async-start(bf16[8,256,128]{2,1,0:T(8,128)(2,1)} %broadcast_in_dim.13), calls=%async_computation.1 | async-start | bytes 1048576 | tf_op jit(solution)/shard_map/all_to_all | solution.py:411
  64.8 12.2 %copy-start = (bf16[1024,1024]{1,0:T(8,128)(2,1)S(1)}, bf16[1024,1024]{1,0:T(8,128)(2,1)}, u32[]{:S(2)}) copy-start(bf16[1024,1024]{1,0:T(8,128)(2,1)} %wout.3) | copy-start | bytes 6291460
  64.8 12.2 %copy-start.1 = (bf16[1024,1024]{1,0:T(8,128)(2,1)S(1)}, bf16[1024,1024]{1,0:T(8,128)(2,1)}, u32[]{:S(2)}) copy-start(bf16[1024,1024]{1,0:T(8,128)(2,1)} %mid.1) | copy-start | bytes 6291460

commit v3 on v2

--- a/solution.py
+++ b/solution.py
@@ -71,7 +71,7 @@
 def local_kernel(
     low, own, high, mask_embed, gain, cgain, embed_hbm, lq, lk, lv, wout_hbm, cq, ck, cv,
     att, payload,
-    hot, logs, scores, probs, pooled_in, matt, embed, local_w, weights, normed, k3, vt, att_out,
+    hot, logs, scores, probs, pooled_in, matt, embed, local_w, weights, normed, k2, vt, att_out,
     sem_e, sem_l, sem_w, sem_o,
 ):
     step = pl.program_id(0)
@@ -147,12 +147,10 @@
     for c in chunks(ROWS):
         k = rounded(k_all[c]) * (math.log2(math.e) * WIDTH**-0.5)
         k_a = k.astype(BF16)
-        rest = k - k_a.astype(F32)
-        k_b = rest.astype(BF16)
-        k_c = (rest - k_b.astype(F32)).astype(BF16)
+        k_b = (k - k_a.astype(F32)).astype(BF16)
         for h in range(GROUP):
             s = slice(h * WIDTH, (h + 1) * WIDTH)
-            k3[h, c] = jnp.concatenate([k_a[:, s], k_b[:, s], k_c[:, s]], axis=1)
+            k2[h, c] = jnp.concatenate([k_a[:, s], k_b[:, s]], axis=1)
     v = rounded(dot(normed[...], local_w[2, step]))
     v_t = v[0:VOCAB].T
     v_m = jnp.broadcast_to(v[VOCAB : VOCAB + 1], (128, COLS)).T
@@ -176,7 +174,7 @@
     def score(u):
         t, h = units[u]
         q_h = queries[t][h * WIDTH : (h + 1) * WIDTH]
-        s = dot(k3[h], jnp.concatenate([q_h, q_h, q_h], axis=0))
+        s = dot(k2[h], jnp.concatenate([q_h, q_h], axis=0))
         top = None
         for c in chunks(ROWS):
             part = s[c] + logs[c, t * TILE : (t + 1) * TILE]
@@ -259,7 +257,7 @@
             pltpu.VMEM((3, steps, D, COLS), BF16),
             pltpu.VMEM((4, D, D), BF16),
             pltpu.VMEM((ROWS, D), BF16),
-            pltpu.VMEM((GROUP, ROWS, 3 * WIDTH), BF16),
+            pltpu.VMEM((GROUP, ROWS, 2 * WIDTH), BF16),
             pltpu.VMEM((GROUP, VROWS, VOCAB), BF16),
             pltpu.VMEM((steps, rows, COLS), BF16),
             pltpu.SemaphoreType.DMA(()),

time: 79.8 us -> 79.5 us (level)
  no operation moved by 1% of the time
where the time goes in v3:
time: 79.5 us; the launch traced here: 79.1 us
  Pallas kernels  34 us (43%)
  blocking collectives  28.8 us (36%)
  starting transfers between devices  7.7 us (10%)
  waiting for transfers between devices  6.33 us (8%)
  local copies, waits for them, and re-layouts  1.49 us (2%)
    pallas_call x1, Pallas kernels, local_attention(): pl.pallas_call(local_kernel, grid=(steps,), in_specs=[whole(x.shape) for...  22.9 us
    all_to_all x1, blocking collectives, body(): lax.all_to_all(payload, PLANE, split_axis=0, concat_axis=0, tiled=True)  17.7 us
    all_to_all x1, blocking collectives, body(): back = lax.all_to_all(mixed, PLANE, split_axis=0, concat_axis=0, tiled=True)  11.1 us
    pallas_call x1, Pallas kernels, make_mid(): pl.pallas_call(mid_kernel, grid=(rows // SUB,), in_specs=[pl.BlockSpec((S...  7.64 us
    all_to_all x1, starting transfers between devices, body(): kv = lax.all_to_all(kv, RING, split_axis=0, concat_axis=0, tiled=True)  5.12 us
    ppermute x1, waiting for transfers between devices, body(): high = lax.ppermute(own[:HALF_WIN], ALL, backward)  3.63 us
    all_to_all x1, waiting for transfers between devices, body(): kv = lax.all_to_all(kv, RING, split_axis=0, concat_axis=0, tiled=True)  2.71 us
    pallas_call x1, Pallas kernels, finish(): pl.pallas_call(final_kernel, grid=(rows // SUB,), in_specs=[whole(back.sh...  2.37 us
  transfers between devices with their start and end apart: 3, of which 2 were waited for; matrix products, arithmetic and copies ran while one was open for 0% of the time, Pallas kernels for 10%

profile of v3, /device:TPU:0, one launch (start us, length us, event | category | flops | bytes accessed | tf_op | source)
XLA Modules:
  0.0 79.1 jit_solution(14345192485650926608)
XLA Ops:
  0.0 0.7 add_select_fusion.own.ids
  0.7 0.0 copy-start.2
  0.7 1.3 %collective-permute-start = (s32[512]{0:T(512)S(1)}, s32[512]{0:T(512)S(1)}, u32[]{:S(2)}, u32[]{:S(2)}) collective-permute-start(s32[512]{0:T(512)S(1)} %get-tuple-element.14), channel_id=1, source_target_pairs={{0,1},{1,2},{2,3},{3,4},{4,5},{5,6},{6,7},{7,8},{8,9},{9,10},{10,1... | collective-permute-start | bytes 6152 | tf_op jit(solution)/shard_map/ppermute | solution.py:398
  2.0 1.3 %collective-permute-start.1 = (s32[512]{0:T(512)S(1)}, s32[512]{0:T(512)S(1)}, u32[]{:S(2)}, u32[]{:S(2)}) collective-permute-start(s32[512]{0:T(512)S(1)} %get-tuple-element.13), channel_id=1, source_target_pairs={{1,0},{2,1},{3,2},{4,3},{5,4},{6,5},{7,6},{8,7},{9,8},{10,9},{11,1... | collective-permute-start | bytes 6152 | tf_op jit(solution)/shard_map/ppermute | solution.py:399
  3.3 0.0 collective-permute-done.low
  3.3 0.0 copy-start.3
  3.3 3.6 %collective-permute-done.1.high = s32[512]{0:T(512)S(1)} collective-permute-done((s32[512]{0:T(512)S(1)}, s32[512]{0:T(512)S(1)}, u32[]{:S(2)}, u32[]{:S(2)}) %collective-permute-start.1) | collective-permute-done | bytes 2080 | tf_op jit(solution)/shard_map/ppermute | solution.py:399
  7.0 0.0 copy-done.2
  7.0 0.0 copy-done.3
  7.0 0.0 copy-start.4
  7.0 0.6 copy-done.4
  7.6 22.9 %local.1 = (bf16[1024,1024]{1,0:T(8,128)(2,1)}, bf16[16,24,128]{2,1,0:T(8,128)(2,1)}) custom-call(s32[512]{0:T(512)} %copy-done.3, s32[1024]{0:T(1024)} %copy-done.2, s32[512]{0:T(512)} %copy-done.4, bf16[1024]{0:T(1024)(128)(2,1)} %mask_embed.3, bf16[1024]{0:T(1024)(128)(2,1)} %gain.1, bf16[1024]{0:T(1024)(128)(2,1)} %cgain.1, bf16[512,1024]{1,0:T(8,128)(2,1)} %embed.1, ...), custom_call_target="tpu_custom_call" | custom-call | flops 8858370048 | bytes 20971520 | tf_op jit(solution)/shard_map/local/pallas_call | solution.py:240
  30.5 17.7 %all_to_all.15 = bf16[16,24,128]{2,1,0:T(8,128)(2,1)S(1)} all-to-all(bf16[16,24,128]{2,1,0:T(8,128)(2,1)} %get-tuple-element.9), channel_id=1, replica_groups=mesh['x_hi'=2,'x_lo'=2,'y_hi'=2,'z_hi'=2,'z_lo'=2,'y_lo'=2,'core'=2] {'x..., dimensions={0} | all-to-all | bytes 196608 | tf_op jit(solution)/shard_map/all_to_all | solution.py:404
  48.2 0.9 %broadcast_in_dim.13 = bf16[8,256,128]{2,1,0:T(8,128)(2,1)} broadcast(bf16[256,128]{1,0:T(8,128)(2,1)S(1)} %bitcast.3), dimensions={1,2} | broadcast | bytes 589824 | tf_op jit(solution)/shard_map/broadcast_in_dim | solution.py:408
  49.1 5.1 %all-to-all-start.1 = ((bf16[8,256,128]{2,1,0:T(8,128)(2,1)}), bf16[8,256,128]{2,1,0:T(8,128)(2,1)S(1)}, u32[]{:S(2)}, u32[]{:S(2)}) async-start(bf16[8,256,128]{2,1,0:T(8,128)(2,1)} %broadcast_in_dim.13), calls=%async_computation.1 | async-start | bytes 1048576 | tf_op jit(solution)/shard_map/all_to_all | solution.py:409
  54.2 7.6 %mid.1 = bf16[1024,1024]{1,0:T(8,128)(2,1)} custom-call(s32[1024]{0:T(1024)} %copy-done.2, bf16[1024,1024]{1,0:T(8,128)(2,1)} %get-tuple-element.10.att, bf16[512,1024]{1,0:T(8,128)(2,1)} %embed.1, bf16[1024]{0:T(1024)(128)(2,1)} %mask_embed.3, bf16[1024,1024]{1,0:T(8,128)(2,1)} %wout.2), custom_call_target="tpu_custom_call" | custom-call | flops 3254779904 | bytes 8388608 | tf_op jit(solution)/shard_map/mid/pallas_call | solution.py:287
  61.8 2.7 %all-to-all-done.1 = bf16[8,256,128]{2,1,0:T(8,128)(2,1)S(1)} async-done(((bf16[8,256,128]{2,1,0:T(8,128)(2,1)}), bf16[8,256,128]{2,1,0:T(8,128)(2,1)S(1)}, u32[]{:S(2)}, u32[]{:S(2)}) %all-to-all-start.1) | async-done | bytes 524320 | tf_op jit(solution)/shard_map/all_to_all | solution.py:409
  64.5 0.0 copy-start
  64.5 0.0 copy-start.1
  64.5 1.1 %coarse.1 = bf16[16,8,128]{2,1,0:T(8,128)(2,1)S(1)} custom-call(bf16[16,8,128]{2,1,0:T(8,128)(2,1)S(1)} %slice.16.q, bf16[2048,128]{1,0:T(8,128)(2,1)S(1)} %bitcast.2), custom_call_target="tpu_custom_call" | custom-call | flops 8000000000 | bytes 16777216 | tf_op jit(solution)/shard_map/coarse/pallas_call | solution.py:324
  65.6 11.1 %all_to_all.16.back = bf16[16,8,128]{2,1,0:T(8,128)(2,1)S(1)} all-to-all(bf16[16,8,128]{2,1,0:T(8,128)(2,1)S(1)} %coarse.1), channel_id=1, replica_groups=mesh['x_hi'=2,'x_lo'=2,'y_hi'=2,'z_hi'=2,'z_lo'=2,'y_lo'=2,'core'=2] {'x..., dimensions={0} | all-to-all | bytes 65536 | tf_op jit(solution)/shard_map/all_to_all | solution.py:413
  76.7 0.0 copy-done
  76.7 0.0 copy-done.1
  76.7 2.4 %finish.1 = bf16[1024,1024]{1,0:T(8,128)(2,1)} custom-call(bf16[16,8,128]{2,1,0:T(8,128)(2,1)S(1)} %all_to_all.16.back, bf16[1024,1024]{1,0:T(8,128)(2,1)S(1)} %copy-done, bf16[1024,1024]{1,0:T(8,128)(2,1)S(1)} %copy-done.1), custom_call_target="tpu_custom_call" | custom-call | tf_op jit(solution)/shard_map/finish/pallas_call | solution.py:361
  (3 shorter events, 0.0 us)
Async XLA Ops:
  0.7 6.2 %copy-start.2 = (s32[1024]{0:T(1024)}, s32[1024]{0:T(1024)S(1)}, u32[]{:S(2)}) copy-start(s32[1024]{0:T(1024)S(1)} %add_select_fusion.own.ids) | copy-start | bytes 12292
  0.7 2.6 %collective-permute-start = (s32[512]{0:T(512)S(1)}, s32[512]{0:T(512)S(1)}, u32[]{:S(2)}, u32[]{:S(2)}) collective-permute-start(s32[512]{0:T(512)S(1)} %get-tuple-element.14), channel_id=1, source_target_pairs={{0,1},{1,2},{2,3},{3,4},{4,5},{5,6},{6,7},{7,8},{8,9},{9,10},{10,1... | collective-permute-start | bytes 6152 | tf_op jit(solution)/shard_map/ppermute | solution.py:398
  2.0 4.9 %collective-permute-start.1 = (s32[512]{0:T(512)S(1)}, s32[512]{0:T(512)S(1)}, u32[]{:S(2)}, u32[]{:S(2)}) collective-permute-start(s32[512]{0:T(512)S(1)} %get-tuple-element.13), channel_id=1, source_target_pairs={{1,0},{2,1},{3,2},{4,3},{5,4},{6,5},{7,6},{8,7},{9,8},{10,9},{11,1... | collective-permute-start | bytes 6152 | tf_op jit(solution)/shard_map/ppermute | solution.py:399
  3.3 3.6 %copy-start.3 = (s32[512]{0:T(512)}, s32[512]{0:T(512)S(1)}, u32[]{:S(2)}) copy-start(s32[512]{0:T(512)S(1)} %collective-permute-done.low) | copy-start | bytes 6148
  7.0 0.6 copy-start.4
  49.1 15.5 %all-to-all-start.1 = ((bf16[8,256,128]{2,1,0:T(8,128)(2,1)}), bf16[8,256,128]{2,1,0:T(8,128)(2,1)S(1)}, u32[]{:S(2)}, u32[]{:S(2)}) async-start(bf16[8,256,128]{2,1,0:T(8,128)(2,1)} %broadcast_in_dim.13), calls=%async_computation.1 | async-start | bytes 1048576 | tf_op jit(solution)/shard_map/all_to_all | solution.py:409
  64.5 12.2 %copy-start = (bf16[1024,1024]{1,0:T(8,128)(2,1)S(1)}, bf16[1024,1024]{1,0:T(8,128)(2,1)}, u32[]{:S(2)}) copy-start(bf16[1024,1024]{1,0:T(8,128)(2,1)} %wout.3) | copy-start | bytes 6291460
  64.5 12.2 %copy-start.1 = (bf16[1024,1024]{1,0:T(8,128)(2,1)S(1)}, bf16[1024,1024]{1,0:T(8,128)(2,1)}, u32[]{:S(2)}) copy-start(bf16[1024,1024]{1,0:T(8,128)(2,1)} %mid.1) | copy-start | bytes 6291460

commit v4 on v3

--- a/solution.py
+++ b/solution.py
@@ -19,7 +19,7 @@
 TILE = 512
 SUB = 256
 CHUNK = 48
-GROUP = 4
+GROUP = 8
 COLS = GROUP * WIDTH
 VROWS = WIDTH + 16
 MIB = 1 << 20
@@ -138,11 +138,11 @@
         row = jnp.broadcast_to(normalize(mask_row, gain_row).astype(F32), (16, D))
         normed[VOCAB:ROWS, :] = jnp.where(keep, row, 0.0).astype(BF16)
 
-    for i in range(3):
-        local_copy(i, step).wait()
+    local_copy(0, step).wait()
     q = rounded(dot(normed[...], local_w[0, step]))
     qt = q[0:VOCAB].T.astype(BF16)
     qm = jnp.broadcast_to(q[VOCAB : VOCAB + 1], (128, COLS)).T
+    local_copy(1, step).wait()
     k_all = dot(normed[...], local_w[1, step])
     for c in chunks(ROWS):
         k = rounded(k_all[c]) * (math.log2(math.e) * WIDTH**-0.5)
@@ -151,6 +151,7 @@
         for h in range(GROUP):
             s = slice(h * WIDTH, (h + 1) * WIDTH)
             k2[h, c] = jnp.concatenate([k_a[:, s], k_b[:, s]], axis=1)
+    local_copy(2, step).wait()
     v = rounded(dot(normed[...], local_w[2, step]))
     v_t = v[0:VOCAB].T
     v_m = jnp.broadcast_to(v[VOCAB : VOCAB + 1], (128, COLS)).T

time: 79.5 us -> 81.6 us (1.026)
  Pallas kernels: 34 us -> 36.1 us
    pallas_call x1, Pallas kernels: 22.9 us -> 25 us  [local_attention(): pl.pallas_call(local_kernel, grid=(steps,), in_specs=[whole(x.shape) for...]
  transfers between devices with their start and end apart: 3 -> 3, of which waited for: 2 -> 2; matrix products, arithmetic and copies ran while one was open for 0% -> 0% of each run, Pallas kernels for 10% -> 9%
where the time goes in v4:
time: 81.6 us; the launch traced here: 81.1 us
  Pallas kernels  36.1 us (44%)
  blocking collectives  28.8 us (35%)
  starting transfers between devices  7.71 us (9%)
  waiting for transfers between devices  6.33 us (8%)
  local copies, waits for them, and re-layouts  1.49 us (2%)
    pallas_call x1, Pallas kernels, local_attention(): pl.pallas_call(local_kernel, grid=(steps,), in_specs=[whole(x.shape) for...  25 us
    all_to_all x1, blocking collectives, body(): lax.all_to_all(payload, PLANE, split_axis=0, concat_axis=0, tiled=True)  17.7 us
    all_to_all x1, blocking collectives, body(): back = lax.all_to_all(mixed, PLANE, split_axis=0, concat_axis=0, tiled=True)  11.1 us
    pallas_call x1, Pallas kernels, make_mid(): pl.pallas_call(mid_kernel, grid=(rows // SUB,), in_specs=[pl.BlockSpec((S...  7.64 us
    all_to_all x1, starting transfers between devices, body(): kv = lax.all_to_all(kv, RING, split_axis=0, concat_axis=0, tiled=True)  5.14 us
    ppermute x1, waiting for transfers between devices, body(): high = lax.ppermute(own[:HALF_WIN], ALL, backward)  3.63 us
    all_to_all x1, waiting for transfers between devices, body(): kv = lax.all_to_all(kv, RING, split_axis=0, concat_axis=0, tiled=True)  2.71 us
    pallas_call x1, Pallas kernels, finish(): pl.pallas_call(final_kernel, grid=(rows // SUB,), in_specs=[whole(back.sh...  2.37 us
  transfers between devices with their start and end apart: 3, of which 2 were waited for; matrix products, arithmetic and copies ran while one was open for 0% of the time, Pallas kernels for 9%

profile of v4, /device:TPU:0, one launch (start us, length us, event | category | flops | bytes accessed | tf_op | source)
XLA Modules:
  0.0 81.1 jit_solution(14318141982356073457)
XLA Ops:
  0.0 0.7 add_select_fusion.own.ids
  0.7 0.0 copy-start.2
  0.7 1.3 %collective-permute-start = (s32[512]{0:T(512)S(1)}, s32[512]{0:T(512)S(1)}, u32[]{:S(2)}, u32[]{:S(2)}) collective-permute-start(s32[512]{0:T(512)S(1)} %get-tuple-element.14), channel_id=1, source_target_pairs={{0,1},{1,2},{2,3},{3,4},{4,5},{5,6},{6,7},{7,8},{8,9},{9,10},{10,1... | collective-permute-start | bytes 6152 | tf_op jit(solution)/shard_map/ppermute | solution.py:399
  2.0 1.3 %collective-permute-start.1 = (s32[512]{0:T(512)S(1)}, s32[512]{0:T(512)S(1)}, u32[]{:S(2)}, u32[]{:S(2)}) collective-permute-start(s32[512]{0:T(512)S(1)} %get-tuple-element.13), channel_id=1, source_target_pairs={{1,0},{2,1},{3,2},{4,3},{5,4},{6,5},{7,6},{8,7},{9,8},{10,9},{11,1... | collective-permute-start | bytes 6152 | tf_op jit(solution)/shard_map/ppermute | solution.py:400
  3.3 0.0 collective-permute-done.low
  3.3 0.0 copy-start.3
  3.3 3.6 %collective-permute-done.1.high = s32[512]{0:T(512)S(1)} collective-permute-done((s32[512]{0:T(512)S(1)}, s32[512]{0:T(512)S(1)}, u32[]{:S(2)}, u32[]{:S(2)}) %collective-permute-start.1) | collective-permute-done | bytes 2080 | tf_op jit(solution)/shard_map/ppermute | solution.py:400
  7.0 0.0 copy-done.2
  7.0 0.0 copy-done.3
  7.0 0.0 copy-start.4
  7.0 0.6 copy-done.4
  7.6 25.0 %local.1 = (bf16[1024,1024]{1,0:T(8,128)(2,1)}, bf16[16,24,128]{2,1,0:T(8,128)(2,1)}) custom-call(s32[512]{0:T(512)} %copy-done.3, s32[1024]{0:T(1024)} %copy-done.2, s32[512]{0:T(512)} %copy-done.4, bf16[1024]{0:T(1024)(128)(2,1)} %mask_embed.3, bf16[1024]{0:T(1024)(128)(2,1)} %gain.1, bf16[1024]{0:T(1024)(128)(2,1)} %cgain.1, bf16[512,1024]{1,0:T(8,128)(2,1)} %embed.1, ...), custom_call_target="tpu_custom_call" | custom-call | flops 8858370048 | bytes 20971520 | tf_op jit(solution)/shard_map/local/pallas_call | solution.py:241
  32.5 17.7 %all_to_all.15 = bf16[16,24,128]{2,1,0:T(8,128)(2,1)S(1)} all-to-all(bf16[16,24,128]{2,1,0:T(8,128)(2,1)} %get-tuple-element.9), channel_id=1, replica_groups=mesh['x_hi'=2,'x_lo'=2,'y_hi'=2,'z_hi'=2,'z_lo'=2,'y_lo'=2,'core'=2] {'x..., dimensions={0} | all-to-all | bytes 196608 | tf_op jit(solution)/shard_map/all_to_all | solution.py:405
  50.2 0.9 %broadcast_in_dim.13 = bf16[8,256,128]{2,1,0:T(8,128)(2,1)} broadcast(bf16[256,128]{1,0:T(8,128)(2,1)S(1)} %bitcast.3), dimensions={1,2} | broadcast | bytes 589824 | tf_op jit(solution)/shard_map/broadcast_in_dim | solution.py:409
  51.1 5.1 %all-to-all-start.1 = ((bf16[8,256,128]{2,1,0:T(8,128)(2,1)}), bf16[8,256,128]{2,1,0:T(8,128)(2,1)S(1)}, u32[]{:S(2)}, u32[]{:S(2)}) async-start(bf16[8,256,128]{2,1,0:T(8,128)(2,1)} %broadcast_in_dim.13), calls=%async_computation.1 | async-start | bytes 1048576 | tf_op jit(solution)/shard_map/all_to_all | solution.py:410
  56.2 7.6 %mid.1 = bf16[1024,1024]{1,0:T(8,128)(2,1)} custom-call(s32[1024]{0:T(1024)} %copy-done.2, bf16[1024,1024]{1,0:T(8,128)(2,1)} %get-tuple-element.10.att, bf16[512,1024]{1,0:T(8,128)(2,1)} %embed.1, bf16[1024]{0:T(1024)(128)(2,1)} %mask_embed.3, bf16[1024,1024]{1,0:T(8,128)(2,1)} %wout.2), custom_call_target="tpu_custom_call" | custom-call | flops 3254779904 | bytes 8388608 | tf_op jit(solution)/shard_map/mid/pallas_call | solution.py:288
  63.9 2.7 %all-to-all-done.1 = bf16[8,256,128]{2,1,0:T(8,128)(2,1)S(1)} async-done(((bf16[8,256,128]{2,1,0:T(8,128)(2,1)}), bf16[8,256,128]{2,1,0:T(8,128)(2,1)S(1)}, u32[]{:S(2)}, u32[]{:S(2)}) %all-to-all-start.1) | async-done | bytes 524320 | tf_op jit(solution)/shard_map/all_to_all | solution.py:410
  66.6 0.0 copy-start
  66.6 0.0 copy-start.1
  66.6 1.1 %coarse.1 = bf16[16,8,128]{2,1,0:T(8,128)(2,1)S(1)} custom-call(bf16[16,8,128]{2,1,0:T(8,128)(2,1)S(1)} %slice.16.q, bf16[2048,128]{1,0:T(8,128)(2,1)S(1)} %bitcast.2), custom_call_target="tpu_custom_call" | custom-call | flops 8000000000 | bytes 16777216 | tf_op jit(solution)/shard_map/coarse/pallas_call | solution.py:325
  67.7 11.1 %all_to_all.16.back = bf16[16,8,128]{2,1,0:T(8,128)(2,1)S(1)} all-to-all(bf16[16,8,128]{2,1,0:T(8,128)(2,1)S(1)} %coarse.1), channel_id=1, replica_groups=mesh['x_hi'=2,'x_lo'=2,'y_hi'=2,'z_hi'=2,'z_lo'=2,'y_lo'=2,'core'=2] {'x..., dimensions={0} | all-to-all | bytes 65536 | tf_op jit(solution)/shard_map/all_to_all | solution.py:414
  78.7 0.0 copy-done
  78.7 0.0 copy-done.1
  78.8 2.4 %finish.1 = bf16[1024,1024]{1,0:T(8,128)(2,1)} custom-call(bf16[16,8,128]{2,1,0:T(8,128)(2,1)S(1)} %all_to_all.16.back, bf16[1024,1024]{1,0:T(8,128)(2,1)S(1)} %copy-done, bf16[1024,1024]{1,0:T(8,128)(2,1)S(1)} %copy-done.1), custom_call_target="tpu_custom_call" | custom-call | tf_op jit(solution)/shard_map/finish/pallas_call | solution.py:362
  (3 shorter events, 0.0 us)
Async XLA Ops:
  0.7 6.2 %copy-start.2 = (s32[1024]{0:T(1024)}, s32[1024]{0:T(1024)S(1)}, u32[]{:S(2)}) copy-start(s32[1024]{0:T(1024)S(1)} %add_select_fusion.own.ids) | copy-start | bytes 12292
  0.7 2.6 %collective-permute-start = (s32[512]{0:T(512)S(1)}, s32[512]{0:T(512)S(1)}, u32[]{:S(2)}, u32[]{:S(2)}) collective-permute-start(s32[512]{0:T(512)S(1)} %get-tuple-element.14), channel_id=1, source_target_pairs={{0,1},{1,2},{2,3},{3,4},{4,5},{5,6},{6,7},{7,8},{8,9},{9,10},{10,1... | collective-permute-start | bytes 6152 | tf_op jit(solution)/shard_map/ppermute | solution.py:399
  2.0 4.9 %collective-permute-start.1 = (s32[512]{0:T(512)S(1)}, s32[512]{0:T(512)S(1)}, u32[]{:S(2)}, u32[]{:S(2)}) collective-permute-start(s32[512]{0:T(512)S(1)} %get-tuple-element.13), channel_id=1, source_target_pairs={{1,0},{2,1},{3,2},{4,3},{5,4},{6,5},{7,6},{8,7},{9,8},{10,9},{11,1... | collective-permute-start | bytes 6152 | tf_op jit(solution)/shard_map/ppermute | solution.py:400
  3.3 3.6 %copy-start.3 = (s32[512]{0:T(512)}, s32[512]{0:T(512)S(1)}, u32[]{:S(2)}) copy-start(s32[512]{0:T(512)S(1)} %collective-permute-done.low) | copy-start | bytes 6148
  7.0 0.6 copy-start.4
  51.1 15.5 %all-to-all-start.1 = ((bf16[8,256,128]{2,1,0:T(8,128)(2,1)}), bf16[8,256,128]{2,1,0:T(8,128)(2,1)S(1)}, u32[]{:S(2)}, u32[]{:S(2)}) async-start(bf16[8,256,128]{2,1,0:T(8,128)(2,1)} %broadcast_in_dim.13), calls=%async_computation.1 | async-start | bytes 1048576 | tf_op jit(solution)/shard_map/all_to_all | solution.py:410
  66.6 12.2 %copy-start = (bf16[1024,1024]{1,0:T(8,128)(2,1)S(1)}, bf16[1024,1024]{1,0:T(8,128)(2,1)}, u32[]{:S(2)}) copy-start(bf16[1024,1024]{1,0:T(8,128)(2,1)} %wout.3) | copy-start | bytes 6291460
  66.6 12.2 %copy-start.1 = (bf16[1024,1024]{1,0:T(8,128)(2,1)S(1)}, bf16[1024,1024]{1,0:T(8,128)(2,1)}, u32[]{:S(2)}) copy-start(bf16[1024,1024]{1,0:T(8,128)(2,1)} %mid.1) | copy-start | bytes 6291460

commit v5 on v3

--- a/solution.py
+++ b/solution.py
@@ -16,7 +16,7 @@
 ROWS = VOCAB + 16
 HALF_WIN = 512
 POOL = 64
-TILE = 512
+TILE = 1024
 SUB = 256
 CHUNK = 48
 GROUP = 4
@@ -71,7 +71,7 @@
 def local_kernel(
     low, own, high, mask_embed, gain, cgain, embed_hbm, lq, lk, lv, wout_hbm, cq, ck, cv,
     att, payload,
-    hot, logs, scores, probs, pooled_in, matt, embed, local_w, weights, normed, k2, vt, att_out,
+    hot, logs, scores, probs, pooled_in, matt, embed, local_w, weights, normed, k2, vt, att_out, held, peak, vt_last, vm_last,
     sem_e, sem_l, sem_w, sem_o,
 ):
     step = pl.program_id(0)
@@ -81,7 +81,8 @@
 
     def local_copy(i, g):
         src = (lq, lk, lv)[i].at[:, pl.ds(pl.multiple_of(g * COLS, COLS), COLS)]
-        return pltpu.make_async_copy(src, local_w.at[i, g], sem_l.at[i, g])
+        dst = local_w.at[g, :, i * COLS : (i + 1) * COLS]
+        return pltpu.make_async_copy(src, dst, sem_l.at[i, g])
 
     late_copies = [
         pltpu.make_async_copy(src, weights.at[i], sem_w.at[i])
@@ -140,18 +141,59 @@
 
     for i in range(3):
         local_copy(i, step).wait()
-    q = rounded(dot(normed[...], local_w[0, step]))
+    tables = dot(normed[...], local_w[step])
+
+    def mix(vt_h, vm_h, slot, top):
+        for c in chunks(ROWS):
+            probs[slot, c] = jnp.exp2((scores[slot, c] - top).astype(BF16))
+        mixed = dot(vt_h, probs[slot, 0:VOCAB])
+        last = probs[slot, VOCAB:ROWS].astype(F32)[0:1]
+        mixed = mixed + jnp.concatenate([vm_h] * (rows // 128), axis=1) * last
+        return mixed[0:WIDTH] * (1.0 / mixed[WIDTH : WIDTH + 1])
+
+    def put(group, pair, even, odd):
+        out = jnp.concatenate([even, odd], axis=0).T
+        cols = slice(pair * 2 * WIDTH, (pair + 1) * 2 * WIDTH)
+        att_out[group, :, cols] = out.astype(BF16)
+        matt[group, :, cols] = jnp.sum(out.reshape(rows // POOL, POOL, 128), axis=1) * (1.0 / POOL)
+
+    def put_last(group):
+        put(group, GROUP // 2 - 1, held[...], mix(vt_last[...], vm_last[...], 1, peak[0:1]))
+
+    put_last(jnp.maximum(step - 1, 0))
+
+    @pl.when(step > 0)
+    def _():
+        out_copy(step - 1).start()
+
+    q = rounded(tables[:, 0:COLS])
     qt = q[0:VOCAB].T.astype(BF16)
     qm = jnp.broadcast_to(q[VOCAB : VOCAB + 1], (128, COLS)).T
-    k_all = dot(normed[...], local_w[1, step])
+    own_cols = slice(HALF_WIN, HALF_WIN + rows)
+    masked = hot[VOCAB:ROWS, own_cols].astype(F32)[0:1]
+    x = dot(qt, hot[0:VOCAB, own_cols])
+    queries = (x + jnp.concatenate([qm] * (rows // 128), axis=1) * masked).astype(BF16)
     for c in chunks(ROWS):
-        k = rounded(k_all[c]) * (math.log2(math.e) * WIDTH**-0.5)
+        k = rounded(tables[c, COLS : 2 * COLS]) * (math.log2(math.e) * WIDTH**-0.5)
         k_a = k.astype(BF16)
         k_b = (k - k_a.astype(F32)).astype(BF16)
         for h in range(GROUP):
             s = slice(h * WIDTH, (h + 1) * WIDTH)
             k2[h, c] = jnp.concatenate([k_a[:, s], k_b[:, s]], axis=1)
-    v = rounded(dot(normed[...], local_w[2, step]))
+
+    def score(h):
+        q_h = queries[h * WIDTH : (h + 1) * WIDTH]
+        s = dot(k2[h], jnp.concatenate([q_h, q_h], axis=0))
+        top = None
+        for c in chunks(ROWS):
+            part = s[c] + logs[c]
+            scores[h % 2, c] = part
+            best = jnp.max(part.reshape((c.stop - c.start) // 8, 8, rows), axis=0)
+            top = best if top is None else jnp.maximum(top, best)
+        return jnp.max(top, axis=0, keepdims=True)
+
+    top = score(0)
+    v = rounded(tables[:, 2 * COLS :])
     v_t = v[0:VOCAB].T
     v_m = jnp.broadcast_to(v[VOCAB : VOCAB + 1], (128, COLS)).T
     ones = jnp.where(lax.broadcasted_iota(jnp.int32, (16, VOCAB), 0) == 0, 1.0, 0.0)
@@ -161,56 +203,24 @@
         vt[h] = jnp.concatenate([v_t[s], ones], axis=0).astype(BF16)
         vm.append(jnp.concatenate([v_m[s], ones[:, 0:128]], axis=0))
 
-    queries = []
-    for t in range(rows // TILE):
-        own_cols = slice(HALF_WIN + t * TILE, HALF_WIN + (t + 1) * TILE)
-        masked = hot[VOCAB:ROWS, own_cols].astype(F32)[0:1]
-        x = dot(qt, hot[0:VOCAB, own_cols])
-        x = x + jnp.concatenate([qm] * (TILE // 128), axis=1) * masked
-        queries.append(x.astype(BF16))
-
-    units = [(t, h) for t in range(rows // TILE) for h in range(GROUP)]
-
-    def score(u):
-        t, h = units[u]
-        q_h = queries[t][h * WIDTH : (h + 1) * WIDTH]
-        s = dot(k2[h], jnp.concatenate([q_h, q_h], axis=0))
-        top = None
-        for c in chunks(ROWS):
-            part = s[c] + logs[c, t * TILE : (t + 1) * TILE]
-            scores[u % 2, c] = part
-            peak = jnp.max(part.reshape((c.stop - c.start) // 8, 8, TILE), axis=0)
-            top = peak if top is None else jnp.maximum(top, peak)
-        return jnp.max(top, axis=0, keepdims=True)
-
-    def mix(u, top):
-        h = units[u][1]
-        for c in chunks(ROWS):
-            probs[u % 2, c] = jnp.exp2((scores[u % 2, c] - top).astype(BF16))
-        mixed = dot(vt[h], probs[u % 2, 0:VOCAB])
-        last = probs[u % 2, VOCAB:ROWS].astype(F32)[0:1]
-        mixed = mixed + jnp.concatenate([vm[h]] * (TILE // 128), axis=1) * last
-        return mixed[0:WIDTH] * (1.0 / mixed[WIDTH : WIDTH + 1])
-
-    top = score(0)
-    held = None
-    for u, (t, h) in enumerate(units):
-        later = score(u + 1) if u + 1 < len(units) else None
-        mixed = mix(u, top)
+    even = None
+    for h in range(GROUP - 1):
+        later = score(h + 1)
+        mixed = mix(vt[h], vm[h], h % 2, top)
         top = later
         if h % 2 == 0:
-            held = mixed
-            continue
-        out = jnp.concatenate([held, mixed], axis=0).T
-        cols = slice((h - 1) * WIDTH, (h + 1) * WIDTH)
-        att_out[step, t * TILE : (t + 1) * TILE, cols] = out.astype(BF16)
-        each = TILE // POOL
-        mean = jnp.sum(out.reshape(each, POOL, 128), axis=1) * (1.0 / POOL)
-        matt[step, t * each : (t + 1) * each, cols] = mean
-    out_copy(step).start()
+            even = mixed
+        else:
+            put(step, h // 2, even, mixed)
+    held[...] = even
+    peak[...] = jnp.broadcast_to(top, peak.shape)
+    vt_last[...] = vt[GROUP - 1]
+    vm_last[...] = vm[GROUP - 1]
 
     @pl.when(step == steps - 1)
     def _():
+        put_last(step)
+        out_copy(step).start()
         for copy in late_copies:
             copy.wait()
         mean = jnp.concatenate([matt[g] for g in range(steps)], axis=1)
@@ -254,12 +264,16 @@
             pltpu.VMEM((16, D), F32),
             pltpu.VMEM((steps, rows // POOL, COLS), F32),
             pltpu.VMEM((VOCAB, D), BF16),
-            pltpu.VMEM((3, steps, D, COLS), BF16),
+            pltpu.VMEM((steps, D, 3 * COLS), BF16),
             pltpu.VMEM((4, D, D), BF16),
             pltpu.VMEM((ROWS, D), BF16),
             pltpu.VMEM((GROUP, ROWS, 2 * WIDTH), BF16),
             pltpu.VMEM((GROUP, VROWS, VOCAB), BF16),
             pltpu.VMEM((steps, rows, COLS), BF16),
+            pltpu.VMEM((WIDTH, rows), F32),
+            pltpu.VMEM((8, rows), F32),
+            pltpu.VMEM((VROWS, VOCAB), BF16),
+            pltpu.VMEM((VROWS, 128), F32),
             pltpu.SemaphoreType.DMA(()),
             pltpu.SemaphoreType.DMA((3, steps)),
             pltpu.SemaphoreType.DMA((4,)),

time: 79.5 us -> 80.9 us (1.018)
  Pallas kernels: 34 us -> 35.4 us
    pallas_call x1, Pallas kernels: 22.9 us -> 24.3 us  [local_attention(): pl.pallas_call(local_kernel, grid=(steps,), in_specs=[whole(x.shape) for...]
  transfers between devices with their start and end apart: 3 -> 3, of which waited for: 2 -> 2; matrix products, arithmetic and copies ran while one was open for 0% -> 0% of each run, Pallas kernels for 10% -> 9%
where the time goes in v5:
time: 80.9 us; the launch traced here: 80.4 us
  Pallas kernels  35.4 us (44%)
  blocking collectives  28.8 us (36%)
  starting transfers between devices  7.72 us (10%)
  waiting for transfers between devices  6.33 us (8%)
  local copies, waits for them, and re-layouts  1.49 us (2%)
    pallas_call x1, Pallas kernels, local_attention(): pl.pallas_call(local_kernel, grid=(steps,), in_specs=[whole(x.shape) for...  24.3 us
    all_to_all x1, blocking collectives, body(): lax.all_to_all(payload, PLANE, split_axis=0, concat_axis=0, tiled=True)  17.7 us
    all_to_all x1, blocking collectives, body(): back = lax.all_to_all(mixed, PLANE, split_axis=0, concat_axis=0, tiled=True)  11.1 us
    pallas_call x1, Pallas kernels, make_mid(): pl.pallas_call(mid_kernel, grid=(rows // SUB,), in_specs=[pl.BlockSpec((S...  7.64 us
    all_to_all x1, starting transfers between devices, body(): kv = lax.all_to_all(kv, RING, split_axis=0, concat_axis=0, tiled=True)  5.14 us
    ppermute x1, waiting for transfers between devices, body(): high = lax.ppermute(own[:HALF_WIN], ALL, backward)  3.63 us
    all_to_all x1, waiting for transfers between devices, body(): kv = lax.all_to_all(kv, RING, split_axis=0, concat_axis=0, tiled=True)  2.71 us
    pallas_call x1, Pallas kernels, finish(): pl.pallas_call(final_kernel, grid=(rows // SUB,), in_specs=[whole(back.sh...  2.37 us
  transfers between devices with their start and end apart: 3, of which 2 were waited for; matrix products, arithmetic and copies ran while one was open for 0% of the time, Pallas kernels for 9%

profile of v5, /device:TPU:0, one launch (start us, length us, event | category | flops | bytes accessed | tf_op | source)
XLA Modules:
  0.0 80.4 jit_solution(52855920061148285)
XLA Ops:
  0.0 0.7 add_select_fusion.own.ids
  0.7 0.0 copy-start.2
  0.7 1.3 %collective-permute-start = (s32[512]{0:T(512)S(1)}, s32[512]{0:T(512)S(1)}, u32[]{:S(2)}, u32[]{:S(2)}) collective-permute-start(s32[512]{0:T(512)S(1)} %get-tuple-element.14), channel_id=1, source_target_pairs={{0,1},{1,2},{2,3},{3,4},{4,5},{5,6},{6,7},{7,8},{8,9},{9,10},{10,1... | collective-permute-start | bytes 6152 | tf_op jit(solution)/shard_map/ppermute | solution.py:412
  2.0 1.3 %collective-permute-start.1 = (s32[512]{0:T(512)S(1)}, s32[512]{0:T(512)S(1)}, u32[]{:S(2)}, u32[]{:S(2)}) collective-permute-start(s32[512]{0:T(512)S(1)} %get-tuple-element.13), channel_id=1, source_target_pairs={{1,0},{2,1},{3,2},{4,3},{5,4},{6,5},{7,6},{8,7},{9,8},{10,9},{11,1... | collective-permute-start | bytes 6152 | tf_op jit(solution)/shard_map/ppermute | solution.py:413
  3.3 0.0 collective-permute-done.low
  3.3 0.0 copy-start.3
  3.3 3.6 %collective-permute-done.1.high = s32[512]{0:T(512)S(1)} collective-permute-done((s32[512]{0:T(512)S(1)}, s32[512]{0:T(512)S(1)}, u32[]{:S(2)}, u32[]{:S(2)}) %collective-permute-start.1) | collective-permute-done | bytes 2080 | tf_op jit(solution)/shard_map/ppermute | solution.py:413
  7.0 0.0 copy-done.2
  7.0 0.0 copy-done.3
  7.0 0.0 copy-start.4
  7.0 0.6 copy-done.4
  7.6 24.3 %local.1 = (bf16[1024,1024]{1,0:T(8,128)(2,1)}, bf16[16,24,128]{2,1,0:T(8,128)(2,1)}) custom-call(s32[512]{0:T(512)} %copy-done.3, s32[1024]{0:T(1024)} %copy-done.2, s32[512]{0:T(512)} %copy-done.4, bf16[1024]{0:T(1024)(128)(2,1)} %mask_embed.3, bf16[1024]{0:T(1024)(128)(2,1)} %gain.1, bf16[1024]{0:T(1024)(128)(2,1)} %cgain.1, bf16[512,1024]{1,0:T(8,128)(2,1)} %embed.1, ...), custom_call_target="tpu_custom_call" | custom-call | flops 8858370048 | bytes 20971520 | tf_op jit(solution)/shard_map/local/pallas_call | solution.py:250
  31.8 17.7 %all_to_all.15 = bf16[16,24,128]{2,1,0:T(8,128)(2,1)S(1)} all-to-all(bf16[16,24,128]{2,1,0:T(8,128)(2,1)} %get-tuple-element.9), channel_id=1, replica_groups=mesh['x_hi'=2,'x_lo'=2,'y_hi'=2,'z_hi'=2,'z_lo'=2,'y_lo'=2,'core'=2] {'x..., dimensions={0} | all-to-all | bytes 196608 | tf_op jit(solution)/shard_map/all_to_all | solution.py:418
  49.5 0.9 %broadcast_in_dim.13 = bf16[8,256,128]{2,1,0:T(8,128)(2,1)} broadcast(bf16[256,128]{1,0:T(8,128)(2,1)S(1)} %bitcast.3), dimensions={1,2} | broadcast | bytes 589824 | tf_op jit(solution)/shard_map/broadcast_in_dim | solution.py:422
  50.4 5.1 %all-to-all-start.1 = ((bf16[8,256,128]{2,1,0:T(8,128)(2,1)}), bf16[8,256,128]{2,1,0:T(8,128)(2,1)S(1)}, u32[]{:S(2)}, u32[]{:S(2)}) async-start(bf16[8,256,128]{2,1,0:T(8,128)(2,1)} %broadcast_in_dim.13), calls=%async_computation.1 | async-start | bytes 1048576 | tf_op jit(solution)/shard_map/all_to_all | solution.py:423
  55.5 7.6 %mid.1 = bf16[1024,1024]{1,0:T(8,128)(2,1)} custom-call(s32[1024]{0:T(1024)} %copy-done.2, bf16[1024,1024]{1,0:T(8,128)(2,1)} %get-tuple-element.10.att, bf16[512,1024]{1,0:T(8,128)(2,1)} %embed.1, bf16[1024]{0:T(1024)(128)(2,1)} %mask_embed.3, bf16[1024,1024]{1,0:T(8,128)(2,1)} %wout.2), custom_call_target="tpu_custom_call" | custom-call | flops 3254779904 | bytes 8388608 | tf_op jit(solution)/shard_map/mid/pallas_call | solution.py:301
  63.2 2.7 %all-to-all-done.1 = bf16[8,256,128]{2,1,0:T(8,128)(2,1)S(1)} async-done(((bf16[8,256,128]{2,1,0:T(8,128)(2,1)}), bf16[8,256,128]{2,1,0:T(8,128)(2,1)S(1)}, u32[]{:S(2)}, u32[]{:S(2)}) %all-to-all-start.1) | async-done | bytes 524320 | tf_op jit(solution)/shard_map/all_to_all | solution.py:423
  65.9 0.0 copy-start
  65.9 0.0 copy-start.1
  65.9 1.1 %coarse.1 = bf16[16,8,128]{2,1,0:T(8,128)(2,1)S(1)} custom-call(bf16[16,8,128]{2,1,0:T(8,128)(2,1)S(1)} %slice.16.q, bf16[2048,128]{1,0:T(8,128)(2,1)S(1)} %bitcast.2), custom_call_target="tpu_custom_call" | custom-call | flops 8000000000 | bytes 16777216 | tf_op jit(solution)/shard_map/coarse/pallas_call | solution.py:338
  67.0 11.1 %all_to_all.16.back = bf16[16,8,128]{2,1,0:T(8,128)(2,1)S(1)} all-to-all(bf16[16,8,128]{2,1,0:T(8,128)(2,1)S(1)} %coarse.1), channel_id=1, replica_groups=mesh['x_hi'=2,'x_lo'=2,'y_hi'=2,'z_hi'=2,'z_lo'=2,'y_lo'=2,'core'=2] {'x..., dimensions={0} | all-to-all | bytes 65536 | tf_op jit(solution)/shard_map/all_to_all | solution.py:427
  78.0 0.0 copy-done
  78.0 0.0 copy-done.1
  78.1 2.4 %finish.1 = bf16[1024,1024]{1,0:T(8,128)(2,1)} custom-call(bf16[16,8,128]{2,1,0:T(8,128)(2,1)S(1)} %all_to_all.16.back, bf16[1024,1024]{1,0:T(8,128)(2,1)S(1)} %copy-done, bf16[1024,1024]{1,0:T(8,128)(2,1)S(1)} %copy-done.1), custom_call_target="tpu_custom_call" | custom-call | tf_op jit(solution)/shard_map/finish/pallas_call | solution.py:375
  (3 shorter events, 0.0 us)
Async XLA Ops:
  0.7 6.2 %copy-start.2 = (s32[1024]{0:T(1024)}, s32[1024]{0:T(1024)S(1)}, u32[]{:S(2)}) copy-start(s32[1024]{0:T(1024)S(1)} %add_select_fusion.own.ids) | copy-start | bytes 12292
  0.7 2.6 %collective-permute-start = (s32[512]{0:T(512)S(1)}, s32[512]{0:T(512)S(1)}, u32[]{:S(2)}, u32[]{:S(2)}) collective-permute-start(s32[512]{0:T(512)S(1)} %get-tuple-element.14), channel_id=1, source_target_pairs={{0,1},{1,2},{2,3},{3,4},{4,5},{5,6},{6,7},{7,8},{8,9},{9,10},{10,1... | collective-permute-start | bytes 6152 | tf_op jit(solution)/shard_map/ppermute | solution.py:412
  2.0 4.9 %collective-permute-start.1 = (s32[512]{0:T(512)S(1)}, s32[512]{0:T(512)S(1)}, u32[]{:S(2)}, u32[]{:S(2)}) collective-permute-start(s32[512]{0:T(512)S(1)} %get-tuple-element.13), channel_id=1, source_target_pairs={{1,0},{2,1},{3,2},{4,3},{5,4},{6,5},{7,6},{8,7},{9,8},{10,9},{11,1... | collective-permute-start | bytes 6152 | tf_op jit(solution)/shard_map/ppermute | solution.py:413
  3.3 3.6 %copy-start.3 = (s32[512]{0:T(512)}, s32[512]{0:T(512)S(1)}, u32[]{:S(2)}) copy-start(s32[512]{0:T(512)S(1)} %collective-permute-done.low) | copy-start | bytes 6148
  7.0 0.6 copy-start.4
  50.4 15.5 %all-to-all-start.1 = ((bf16[8,256,128]{2,1,0:T(8,128)(2,1)}), bf16[8,256,128]{2,1,0:T(8,128)(2,1)S(1)}, u32[]{:S(2)}, u32[]{:S(2)}) async-start(bf16[8,256,128]{2,1,0:T(8,128)(2,1)} %broadcast_in_dim.13), calls=%async_computation.1 | async-start | bytes 1048576 | tf_op jit(solution)/shard_map/all_to_all | solution.py:423
  65.9 12.2 %copy-start = (bf16[1024,1024]{1,0:T(8,128)(2,1)S(1)}, bf16[1024,1024]{1,0:T(8,128)(2,1)}, u32[]{:S(2)}) copy-start(bf16[1024,1024]{1,0:T(8,128)(2,1)} %wout.3) | copy-start | bytes 6291460
  65.9 12.2 %copy-start.1 = (bf16[1024,1024]{1,0:T(8,128)(2,1)S(1)}, bf16[1024,1024]{1,0:T(8,128)(2,1)}, u32[]{:S(2)}) copy-start(bf16[1024,1024]{1,0:T(8,128)(2,1)} %mid.1) | copy-start | bytes 6291460

commit v6 on v3

--- a/solution.py
+++ b/solution.py
@@ -393,10 +393,11 @@
     rows = token_ids.shape[0]
     own = jnp.where(bar_mask == 1, VOCAB + 1, token_ids + 1)
     count = lax.axis_size(ALL)
-    forward = [(i, i + 1) for i in range(count - 1)]
+    here = lax.axis_index(ALL)
+    forward = [(i, (i + 1) % count) for i in range(count)]
     backward = [(b, a) for a, b in forward]
-    low = lax.ppermute(own[rows - HALF_WIN :], ALL, forward)
-    high = lax.ppermute(own[:HALF_WIN], ALL, backward)
+    low = lax.ppermute(jnp.where(here == count - 1, 0, own[rows - HALF_WIN :]), ALL, forward)
+    high = lax.ppermute(jnp.where(here == 0, 0, own[:HALF_WIN]), ALL, backward)
     att, payload = local_attention(
         low, own, high, mask_embed, local_gain, coarse_gain, embed,
         local_query, local_key, local_value, local_out, coarse_query, coarse_key, coarse_value,

time: 79.5 us -> 76.8 us (0.966)
  blocking collectives: 28.8 us -> 22.3 us
  starting transfers between devices: 7.7 us -> 13.4 us
  waiting for transfers between devices: 6.33 us -> 4.01 us
    all_to_all x1, blocking collectives: 17.7 us -> 11.2 us  [body(): lax.all_to_all(payload, PLANE, split_axis=0, concat_axis=0, tiled=True)]
    ppermute x2, starting transfers between devices: 2.58 us -> 8.35 us  [the longest x1 8.27 us: body(): high = lax.ppermute(jnp.where(here == 0, 0, own[:HALF_WIN]), ALL, backward)]
    ppermute x2, waiting for transfers between devices: 3.63 us -> 1.31 us  [the longest x1 1.19 us: body(): lax.ppermute(jnp.where(here == count - 1, 0, own[rows - HALF_WIN:]), ALL,...]
  transfers between devices with their start and end apart: 3 -> 3, of which waited for: 2 -> 3; matrix products, arithmetic and copies ran while one was open for 0% -> 0% of each run, Pallas kernels for 10% -> 10%
where the time goes in v6:
time: 76.8 us; the launch traced here: 76.4 us
  Pallas kernels  34 us (44%)
  blocking collectives  22.3 us (29%)
  starting transfers between devices  13.4 us (17%)
  waiting for transfers between devices  4.01 us (5%)
  local copies, waits for them, and re-layouts  1.94 us (3%)
    pallas_call x1, Pallas kernels, local_attention(): pl.pallas_call(local_kernel, grid=(steps,), in_specs=[whole(x.shape) for...  22.9 us
    all_to_all x1, blocking collectives, body(): lax.all_to_all(payload, PLANE, split_axis=0, concat_axis=0, tiled=True)  11.2 us
    all_to_all x1, blocking collectives, body(): back = lax.all_to_all(mixed, PLANE, split_axis=0, concat_axis=0, tiled=True)  11.1 us
    ppermute x1, starting transfers between devices, body(): high = lax.ppermute(jnp.where(here == 0, 0, own[:HALF_WIN]), ALL, backward)  8.27 us
    pallas_call x1, Pallas kernels, make_mid(): pl.pallas_call(mid_kernel, grid=(rows // SUB,), in_specs=[pl.BlockSpec((S...  7.64 us
    all_to_all x1, starting transfers between devices, body(): kv = lax.all_to_all(kv, RING, split_axis=0, concat_axis=0, tiled=True)  5.06 us
    all_to_all x1, waiting for transfers between devices, body(): kv = lax.all_to_all(kv, RING, split_axis=0, concat_axis=0, tiled=True)  2.71 us
    pallas_call x1, Pallas kernels, finish(): pl.pallas_call(final_kernel, grid=(rows // SUB,), in_specs=[whole(back.sh...  2.37 us
  transfers between devices with their start and end apart: 3, of which 3 were waited for; matrix products, arithmetic and copies ran while one was open for 0% of the time, Pallas kernels for 10%

profile of v6, /device:TPU:0, one launch (start us, length us, event | category | flops | bytes accessed | tf_op | source)
XLA Modules:
  0.0 76.4 jit_solution(4859242657076318685)
XLA Ops:
  0.0 0.7 add_select_fusion.own.ids
  0.7 0.0 copy-start.2
  0.7 0.1 collective-permute-start
  0.8 8.3 %collective-permute-start.1 = (s32[512]{0:T(512)S(1)}, s32[512]{0:T(512)S(1)}, u32[]{:S(2)}, u32[]{:S(2)}) collective-permute-start(s32[512]{0:T(512)S(1)} %get-tuple-element.13), channel_id=1, source_target_pairs={{1,0},{2,1},{3,2},{4,3},{5,4},{6,5},{7,6},{8,7},{9,8},{10,9},{11,1... | collective-permute-start | bytes 6152 | tf_op jit(solution)/shard_map/ppermute | solution.py:400
  9.1 1.2 %collective-permute-done.low = s32[512]{0:T(512)S(1)} collective-permute-done((s32[512]{0:T(512)S(1)}, s32[512]{0:T(512)S(1)}, u32[]{:S(2)}, u32[]{:S(2)}) %collective-permute-start) | collective-permute-done | bytes 2080 | tf_op jit(solution)/shard_map/ppermute | solution.py:399
  10.3 0.0 copy-start.3
  10.3 0.1 collective-permute-done.1.high
  10.4 0.0 copy-done.2
  10.4 0.5 copy-done.3
  10.8 0.0 copy-start.4
  10.8 0.6 copy-done.4
  11.4 22.9 %local.1 = (bf16[1024,1024]{1,0:T(8,128)(2,1)}, bf16[16,24,128]{2,1,0:T(8,128)(2,1)}) custom-call(s32[512]{0:T(512)} %copy-done.3, s32[1024]{0:T(1024)} %copy-done.2, s32[512]{0:T(512)} %copy-done.4, bf16[1024]{0:T(1024)(128)(2,1)} %mask_embed.3, bf16[1024]{0:T(1024)(128)(2,1)} %gain.1, bf16[1024]{0:T(1024)(128)(2,1)} %cgain.1, bf16[512,1024]{1,0:T(8,128)(2,1)} %embed.1, ...), custom_call_target="tpu_custom_call" | custom-call | flops 8858370048 | bytes 20971520 | tf_op jit(solution)/shard_map/local/pallas_call | solution.py:240
  34.4 11.2 %all_to_all.15 = bf16[16,24,128]{2,1,0:T(8,128)(2,1)S(1)} all-to-all(bf16[16,24,128]{2,1,0:T(8,128)(2,1)} %get-tuple-element.9), channel_id=1, replica_groups=mesh['x_hi'=2,'x_lo'=2,'y_hi'=2,'z_hi'=2,'z_lo'=2,'y_lo'=2,'core'=2] {'x..., dimensions={0} | all-to-all | bytes 196608 | tf_op jit(solution)/shard_map/all_to_all | solution.py:405
  45.6 0.9 %broadcast_in_dim.19 = bf16[8,256,128]{2,1,0:T(8,128)(2,1)} broadcast(bf16[256,128]{1,0:T(8,128)(2,1)S(1)} %bitcast.3), dimensions={1,2} | broadcast | bytes 589824 | tf_op jit(solution)/shard_map/broadcast_in_dim | solution.py:409
  46.4 5.1 %all-to-all-start.1 = ((bf16[8,256,128]{2,1,0:T(8,128)(2,1)}), bf16[8,256,128]{2,1,0:T(8,128)(2,1)S(1)}, u32[]{:S(2)}, u32[]{:S(2)}) async-start(bf16[8,256,128]{2,1,0:T(8,128)(2,1)} %broadcast_in_dim.19), calls=%async_computation.1 | async-start | bytes 1048576 | tf_op jit(solution)/shard_map/all_to_all | solution.py:410
  51.5 7.6 %mid.1 = bf16[1024,1024]{1,0:T(8,128)(2,1)} custom-call(s32[1024]{0:T(1024)} %copy-done.2, bf16[1024,1024]{1,0:T(8,128)(2,1)} %get-tuple-element.10.att, bf16[512,1024]{1,0:T(8,128)(2,1)} %embed.1, bf16[1024]{0:T(1024)(128)(2,1)} %mask_embed.3, bf16[1024,1024]{1,0:T(8,128)(2,1)} %wout.2), custom_call_target="tpu_custom_call" | custom-call | flops 3254779904 | bytes 8388608 | tf_op jit(solution)/shard_map/mid/pallas_call | solution.py:287
  59.1 2.7 %all-to-all-done.1 = bf16[8,256,128]{2,1,0:T(8,128)(2,1)S(1)} async-done(((bf16[8,256,128]{2,1,0:T(8,128)(2,1)}), bf16[8,256,128]{2,1,0:T(8,128)(2,1)S(1)}, u32[]{:S(2)}, u32[]{:S(2)}) %all-to-all-start.1) | async-done | bytes 524320 | tf_op jit(solution)/shard_map/all_to_all | solution.py:410
  61.8 0.0 copy-start
  61.8 0.0 copy-start.1
  61.8 1.1 %coarse.1 = bf16[16,8,128]{2,1,0:T(8,128)(2,1)S(1)} custom-call(bf16[16,8,128]{2,1,0:T(8,128)(2,1)S(1)} %slice.16.q, bf16[2048,128]{1,0:T(8,128)(2,1)S(1)} %bitcast.2), custom_call_target="tpu_custom_call" | custom-call | flops 8000000000 | bytes 16777216 | tf_op jit(solution)/shard_map/coarse/pallas_call | solution.py:324
  62.9 11.1 %all_to_all.16.back = bf16[16,8,128]{2,1,0:T(8,128)(2,1)S(1)} all-to-all(bf16[16,8,128]{2,1,0:T(8,128)(2,1)S(1)} %coarse.1), channel_id=1, replica_groups=mesh['x_hi'=2,'x_lo'=2,'y_hi'=2,'z_hi'=2,'z_lo'=2,'y_lo'=2,'core'=2] {'x..., dimensions={0} | all-to-all | bytes 65536 | tf_op jit(solution)/shard_map/all_to_all | solution.py:414
  74.0 0.0 copy-done
  74.0 0.0 copy-done.1
  74.0 2.4 %finish.1 = bf16[1024,1024]{1,0:T(8,128)(2,1)} custom-call(bf16[16,8,128]{2,1,0:T(8,128)(2,1)S(1)} %all_to_all.16.back, bf16[1024,1024]{1,0:T(8,128)(2,1)S(1)} %copy-done, bf16[1024,1024]{1,0:T(8,128)(2,1)S(1)} %copy-done.1), custom_call_target="tpu_custom_call" | custom-call | tf_op jit(solution)/shard_map/finish/pallas_call | solution.py:361
  (3 shorter events, 0.0 us)
Async XLA Ops:
  0.7 9.7 %copy-start.2 = (s32[1024]{0:T(1024)}, s32[1024]{0:T(1024)S(1)}, u32[]{:S(2)}) copy-start(s32[1024]{0:T(1024)S(1)} %add_select_fusion.own.ids) | copy-start | bytes 12292
  0.7 9.5 %collective-permute-start = (s32[512]{0:T(512)S(1)}, s32[512]{0:T(512)S(1)}, u32[]{:S(2)}, u32[]{:S(2)}) collective-permute-start(s32[512]{0:T(512)S(1)} %get-tuple-element.14), channel_id=1, source_target_pairs={{0,1},{1,2},{2,3},{3,4},{4,5},{5,6},{6,7},{7,8},{8,9},{9,10},{10,1... | collective-permute-start | bytes 6152 | tf_op jit(solution)/shard_map/ppermute | solution.py:399
  0.8 9.6 %collective-permute-start.1 = (s32[512]{0:T(512)S(1)}, s32[512]{0:T(512)S(1)}, u32[]{:S(2)}, u32[]{:S(2)}) collective-permute-start(s32[512]{0:T(512)S(1)} %get-tuple-element.13), channel_id=1, source_target_pairs={{1,0},{2,1},{3,2},{4,3},{5,4},{6,5},{7,6},{8,7},{9,8},{10,9},{11,1... | collective-permute-start | bytes 6152 | tf_op jit(solution)/shard_map/ppermute | solution.py:400
  10.3 0.6 copy-start.3
  10.8 0.6 copy-start.4
  46.4 15.4 %all-to-all-start.1 = ((bf16[8,256,128]{2,1,0:T(8,128)(2,1)}), bf16[8,256,128]{2,1,0:T(8,128)(2,1)S(1)}, u32[]{:S(2)}, u32[]{:S(2)}) async-start(bf16[8,256,128]{2,1,0:T(8,128)(2,1)} %broadcast_in_dim.19), calls=%async_computation.1 | async-start | bytes 1048576 | tf_op jit(solution)/shard_map/all_to_all | solution.py:410
  61.8 12.2 %copy-start = (bf16[1024,1024]{1,0:T(8,128)(2,1)S(1)}, bf16[1024,1024]{1,0:T(8,128)(2,1)}, u32[]{:S(2)}) copy-start(bf16[1024,1024]{1,0:T(8,128)(2,1)} %wout.3) | copy-start | bytes 6291460
  61.8 12.2 %copy-start.1 = (bf16[1024,1024]{1,0:T(8,128)(2,1)S(1)}, bf16[1024,1024]{1,0:T(8,128)(2,1)}, u32[]{:S(2)}) copy-start(bf16[1024,1024]{1,0:T(8,128)(2,1)} %mid.1) | copy-start | bytes 6291460

commit v7 on v6

--- a/solution.py
+++ b/solution.py
@@ -105,18 +105,13 @@
             part = own[c : c + HALF_WIN].reshape(1, HALF_WIN)
             fill_one_hot(hot, HALF_WIN + c, part)
         fill_one_hot(hot, HALF_WIN + rows, high[...].reshape(1, HALF_WIN))
-        j = lax.broadcasted_iota(jnp.int32, (SUB, SUB), 0)
-        i = lax.broadcasted_iota(jnp.int32, (SUB, SUB), 1)
-        first = jnp.where(j >= i, 1.0, 0.0).astype(BF16)
-        last = jnp.where(j <= i, 1.0, 0.0).astype(BF16)
-        every = jnp.ones((SUB, SUB), BF16)
-        span = 2 * HALF_WIN // SUB
+        near = SUB + 2 * HALF_WIN
+        ahead = lax.broadcasted_iota(jnp.int32, (near, SUB), 0) - lax.broadcasted_iota(
+            jnp.int32, (near, SUB), 1
+        )
+        band = jnp.where((ahead >= 0) & (ahead <= 2 * HALF_WIN), 1.0, 0.0).astype(BF16)
         for t in range(rows // SUB):
-            block = lambda b: hot[:, (t + b) * SUB : (t + b + 1) * SUB]
-            inner = block(1)
-            for b in range(2, span):
-                inner = inner + block(b)
-            count = dot(block(0), first) + dot(inner, every) + dot(block(span), last)
+            count = dot(hot[:, t * SUB : t * SUB + near], band)
             for s in chunks(ROWS):
                 c = count[s]
                 logs[s, t * SUB : (t + 1) * SUB] = jnp.where(

time: 76.8 us -> 76.8 us (level)
  no operation moved by 1% of the time
where the time goes in v7:
time: 76.8 us; the launch traced here: 76.4 us
  Pallas kernels  34 us (44%)
  blocking collectives  22.3 us (29%)
  starting transfers between devices  13.4 us (17%)
  waiting for transfers between devices  4.01 us (5%)
  local copies, waits for them, and re-layouts  1.94 us (3%)
    pallas_call x1, Pallas kernels, local_attention(): pl.pallas_call(local_kernel, grid=(steps,), in_specs=[whole(x.shape) for...  22.9 us
    all_to_all x1, blocking collectives, body(): lax.all_to_all(payload, PLANE, split_axis=0, concat_axis=0, tiled=True)  11.2 us
    all_to_all x1, blocking collectives, body(): back = lax.all_to_all(mixed, PLANE, split_axis=0, concat_axis=0, tiled=True)  11.1 us
    ppermute x1, starting transfers between devices, body(): high = lax.ppermute(jnp.where(here == 0, 0, own[:HALF_WIN]), ALL, backward)  8.27 us
    pallas_call x1, Pallas kernels, make_mid(): pl.pallas_call(mid_kernel, grid=(rows // SUB,), in_specs=[pl.BlockSpec((S...  7.64 us
    all_to_all x1, starting transfers between devices, body(): kv = lax.all_to_all(kv, RING, split_axis=0, concat_axis=0, tiled=True)  5.05 us
    all_to_all x1, waiting for transfers between devices, body(): kv = lax.all_to_all(kv, RING, split_axis=0, concat_axis=0, tiled=True)  2.71 us
    pallas_call x1, Pallas kernels, finish(): pl.pallas_call(final_kernel, grid=(rows // SUB,), in_specs=[whole(back.sh...  2.37 us
  transfers between devices with their start and end apart: 3, of which 3 were waited for; matrix products, arithmetic and copies ran while one was open for 0% of the time, Pallas kernels for 10%

profile of v7, /device:TPU:0, one launch (start us, length us, event | category | flops | bytes accessed | tf_op | source)
XLA Modules:
  0.0 76.4 jit_solution(8991512945702044050)
XLA Ops:
  0.0 0.7 add_select_fusion.own.ids
  0.7 0.0 copy-start.2
  0.7 0.1 collective-permute-start
  0.8 8.3 %collective-permute-start.1 = (s32[512]{0:T(512)S(1)}, s32[512]{0:T(512)S(1)}, u32[]{:S(2)}, u32[]{:S(2)}) collective-permute-start(s32[512]{0:T(512)S(1)} %get-tuple-element.13), channel_id=1, source_target_pairs={{1,0},{2,1},{3,2},{4,3},{5,4},{6,5},{7,6},{8,7},{9,8},{10,9},{11,1... | collective-permute-start | bytes 6152 | tf_op jit(solution)/shard_map/ppermute | solution.py:395
  9.1 1.2 %collective-permute-done.low = s32[512]{0:T(512)S(1)} collective-permute-done((s32[512]{0:T(512)S(1)}, s32[512]{0:T(512)S(1)}, u32[]{:S(2)}, u32[]{:S(2)}) %collective-permute-start) | collective-permute-done | bytes 2080 | tf_op jit(solution)/shard_map/ppermute | solution.py:394
  10.3 0.0 copy-start.3
  10.3 0.1 collective-permute-done.1.high
  10.4 0.0 copy-done.2
  10.4 0.5 copy-done.3
  10.8 0.0 copy-start.4
  10.8 0.6 copy-done.4
  11.4 22.9 %local.1 = (bf16[1024,1024]{1,0:T(8,128)(2,1)}, bf16[16,24,128]{2,1,0:T(8,128)(2,1)}) custom-call(s32[512]{0:T(512)} %copy-done.3, s32[1024]{0:T(1024)} %copy-done.2, s32[512]{0:T(512)} %copy-done.4, bf16[1024]{0:T(1024)(128)(2,1)} %mask_embed.3, bf16[1024]{0:T(1024)(128)(2,1)} %gain.1, bf16[1024]{0:T(1024)(128)(2,1)} %cgain.1, bf16[512,1024]{1,0:T(8,128)(2,1)} %embed.1, ...), custom_call_target="tpu_custom_call" | custom-call | flops 8858370048 | bytes 20971520 | tf_op jit(solution)/shard_map/local/pallas_call | solution.py:235
  34.4 11.2 %all_to_all.15 = bf16[16,24,128]{2,1,0:T(8,128)(2,1)S(1)} all-to-all(bf16[16,24,128]{2,1,0:T(8,128)(2,1)} %get-tuple-element.9), channel_id=1, replica_groups=mesh['x_hi'=2,'x_lo'=2,'y_hi'=2,'z_hi'=2,'z_lo'=2,'y_lo'=2,'core'=2] {'x..., dimensions={0} | all-to-all | bytes 196608 | tf_op jit(solution)/shard_map/all_to_all | solution.py:400
  45.6 0.9 %broadcast_in_dim.19 = bf16[8,256,128]{2,1,0:T(8,128)(2,1)} broadcast(bf16[256,128]{1,0:T(8,128)(2,1)S(1)} %bitcast.3), dimensions={1,2} | broadcast | bytes 589824 | tf_op jit(solution)/shard_map/broadcast_in_dim | solution.py:404
  46.4 5.0 %all-to-all-start.1 = ((bf16[8,256,128]{2,1,0:T(8,128)(2,1)}), bf16[8,256,128]{2,1,0:T(8,128)(2,1)S(1)}, u32[]{:S(2)}, u32[]{:S(2)}) async-start(bf16[8,256,128]{2,1,0:T(8,128)(2,1)} %broadcast_in_dim.19), calls=%async_computation.1 | async-start | bytes 1048576 | tf_op jit(solution)/shard_map/all_to_all | solution.py:405
  51.5 7.6 %mid.1 = bf16[1024,1024]{1,0:T(8,128)(2,1)} custom-call(s32[1024]{0:T(1024)} %copy-done.2, bf16[1024,1024]{1,0:T(8,128)(2,1)} %get-tuple-element.10.att, bf16[512,1024]{1,0:T(8,128)(2,1)} %embed.1, bf16[1024]{0:T(1024)(128)(2,1)} %mask_embed.3, bf16[1024,1024]{1,0:T(8,128)(2,1)} %wout.2), custom_call_target="tpu_custom_call" | custom-call | flops 3254779904 | bytes 8388608 | tf_op jit(solution)/shard_map/mid/pallas_call | solution.py:282
  59.1 2.7 %all-to-all-done.1 = bf16[8,256,128]{2,1,0:T(8,128)(2,1)S(1)} async-done(((bf16[8,256,128]{2,1,0:T(8,128)(2,1)}), bf16[8,256,128]{2,1,0:T(8,128)(2,1)S(1)}, u32[]{:S(2)}, u32[]{:S(2)}) %all-to-all-start.1) | async-done | bytes 524320 | tf_op jit(solution)/shard_map/all_to_all | solution.py:405
  61.8 0.0 copy-start
  61.8 0.0 copy-start.1
  61.8 1.1 %coarse.1 = bf16[16,8,128]{2,1,0:T(8,128)(2,1)S(1)} custom-call(bf16[16,8,128]{2,1,0:T(8,128)(2,1)S(1)} %slice.16.q, bf16[2048,128]{1,0:T(8,128)(2,1)S(1)} %bitcast.2), custom_call_target="tpu_custom_call" | custom-call | flops 8000000000 | bytes 16777216 | tf_op jit(solution)/shard_map/coarse/pallas_call | solution.py:319
  62.9 11.1 %all_to_all.16.back = bf16[16,8,128]{2,1,0:T(8,128)(2,1)S(1)} all-to-all(bf16[16,8,128]{2,1,0:T(8,128)(2,1)S(1)} %coarse.1), channel_id=1, replica_groups=mesh['x_hi'=2,'x_lo'=2,'y_hi'=2,'z_hi'=2,'z_lo'=2,'y_lo'=2,'core'=2] {'x..., dimensions={0} | all-to-all | bytes 65536 | tf_op jit(solution)/shard_map/all_to_all | solution.py:409
  74.0 0.0 copy-done
  74.0 0.0 copy-done.1
  74.0 2.4 %finish.1 = bf16[1024,1024]{1,0:T(8,128)(2,1)} custom-call(bf16[16,8,128]{2,1,0:T(8,128)(2,1)S(1)} %all_to_all.16.back, bf16[1024,1024]{1,0:T(8,128)(2,1)S(1)} %copy-done, bf16[1024,1024]{1,0:T(8,128)(2,1)S(1)} %copy-done.1), custom_call_target="tpu_custom_call" | custom-call | tf_op jit(solution)/shard_map/finish/pallas_call | solution.py:356
  (3 shorter events, 0.0 us)
Async XLA Ops:
  0.7 9.7 %copy-start.2 = (s32[1024]{0:T(1024)}, s32[1024]{0:T(1024)S(1)}, u32[]{:S(2)}) copy-start(s32[1024]{0:T(1024)S(1)} %add_select_fusion.own.ids) | copy-start | bytes 12292
  0.7 9.5 %collective-permute-start = (s32[512]{0:T(512)S(1)}, s32[512]{0:T(512)S(1)}, u32[]{:S(2)}, u32[]{:S(2)}) collective-permute-start(s32[512]{0:T(512)S(1)} %get-tuple-element.14), channel_id=1, source_target_pairs={{0,1},{1,2},{2,3},{3,4},{4,5},{5,6},{6,7},{7,8},{8,9},{9,10},{10,1... | collective-permute-start | bytes 6152 | tf_op jit(solution)/shard_map/ppermute | solution.py:394
  0.8 9.6 %collective-permute-start.1 = (s32[512]{0:T(512)S(1)}, s32[512]{0:T(512)S(1)}, u32[]{:S(2)}, u32[]{:S(2)}) collective-permute-start(s32[512]{0:T(512)S(1)} %get-tuple-element.13), channel_id=1, source_target_pairs={{1,0},{2,1},{3,2},{4,3},{5,4},{6,5},{7,6},{8,7},{9,8},{10,9},{11,1... | collective-permute-start | bytes 6152 | tf_op jit(solution)/shard_map/ppermute | solution.py:395
  10.3 0.6 copy-start.3
  10.8 0.6 copy-start.4
  46.4 15.4 %all-to-all-start.1 = ((bf16[8,256,128]{2,1,0:T(8,128)(2,1)}), bf16[8,256,128]{2,1,0:T(8,128)(2,1)S(1)}, u32[]{:S(2)}, u32[]{:S(2)}) async-start(bf16[8,256,128]{2,1,0:T(8,128)(2,1)} %broadcast_in_dim.19), calls=%async_computation.1 | async-start | bytes 1048576 | tf_op jit(solution)/shard_map/all_to_all | solution.py:405
  61.8 12.2 %copy-start = (bf16[1024,1024]{1,0:T(8,128)(2,1)S(1)}, bf16[1024,1024]{1,0:T(8,128)(2,1)}, u32[]{:S(2)}) copy-start(bf16[1024,1024]{1,0:T(8,128)(2,1)} %wout.3) | copy-start | bytes 6291460
  61.8 12.2 %copy-start.1 = (bf16[1024,1024]{1,0:T(8,128)(2,1)S(1)}, bf16[1024,1024]{1,0:T(8,128)(2,1)}, u32[]{:S(2)}) copy-start(bf16[1024,1024]{1,0:T(8,128)(2,1)} %mid.1) | copy-start | bytes 6291460

commit v8 on v6

--- a/solution.py
+++ b/solution.py
@@ -61,11 +61,6 @@
     for s in chunks(ROWS):
         event = lax.broadcasted_iota(jnp.int32, (s.stop - s.start, count), 0) + (s.start + 1)
         out[s, first : first + count] = jnp.where(event == ids, 1.0, 0.0).astype(BF16)
-
-
-def one_hot(ids):
-    event = lax.broadcasted_iota(jnp.int32, (ROWS, ids.shape[1]), 0) + 1
-    return jnp.where(event == ids, 1.0, 0.0).astype(BF16)
 
 
 def local_kernel(
@@ -273,35 +268,65 @@
     )(*small, *arrays)
 
 
-def mid_kernel(ids, att, embed, mask_embed, wout, mid):
-    hot = one_hot(ids[...].reshape(1, SUB))
-    total = dot(att[...], wout[...]) + dot_tn(hot[0:VOCAB], embed[...])
-    row = jnp.broadcast_to(mask_embed[...].reshape(1, D), (16, D))
-    total = total + dot_tn(hot[VOCAB:ROWS], row)
-    mid[...] = total.astype(BF16)
+def mid_kernel(
+    ids, mask_embed, embed_hbm, wout_hbm, att_hbm, mid_hbm, total, embed, wout, att, out, sems
+):
+    rows = att.shape[0]
+    tiles = [slice(c, c + SUB) for c in range(0, rows, SUB)]
+    embed_copy = pltpu.make_async_copy(embed_hbm, embed, sems.at[0])
+    wout_copy = pltpu.make_async_copy(wout_hbm, wout, sems.at[1])
+    att_copies = [
+        pltpu.make_async_copy(att_hbm.at[s], att.at[s], sems.at[2 + t])
+        for t, s in enumerate(tiles)
+    ]
+    out_copies = [
+        pltpu.make_async_copy(out.at[s], mid_hbm.at[s], sems.at[2 + len(tiles) + t])
+        for t, s in enumerate(tiles)
+    ]
+    for copy in [embed_copy, wout_copy] + att_copies:
+        copy.start()
+    own = jnp.broadcast_to(ids[...].reshape(1, rows).astype(F32), (128, rows)).T
+    lane = lax.broadcasted_iota(jnp.int32, (SUB, 128), 1).astype(F32)
+    mask_row = mask_embed[...].reshape(1, D).astype(F32)
+    embed_copy.wait()
+    for s in tiles:
+        hot = [jnp.where(own[s] == lane + (b + 1), 1.0, 0.0) for b in range(0, VOCAB, 128)]
+        hot = jnp.concatenate(hot, axis=1).astype(BF16)
+        masked = jnp.where(own[s] == VOCAB + 1.0, 1.0, 0.0)
+        masked = jnp.concatenate([masked] * (D // 128), axis=1)
+        total[s, :] = dot(hot, embed[...]) + masked * mask_row
+    wout_copy.wait()
+    for t, s in enumerate(tiles):
+        att_copies[t].wait()
+        out[s, :] = (total[s, :] + dot(att[s, :], wout[...])).astype(BF16)
+        out_copies[t].start()
+    for copy in out_copies:
+        copy.wait()
 
 
 def make_mid(ids, att, embed, mask_embed, wout):
     rows = att.shape[0]
-    whole = lambda shape: pl.BlockSpec(shape, lambda g: (0,) * len(shape))
+    vmem = pl.BlockSpec(memory_space=pltpu.VMEM)
+    hbm = pl.BlockSpec(memory_space=pl.ANY)
     return pl.pallas_call(
         mid_kernel,
-        grid=(rows // SUB,),
-        in_specs=[
-            pl.BlockSpec((SUB,), lambda g: (g,)),
-            pl.BlockSpec((SUB, D), lambda g: (g, 0)),
-            whole((VOCAB, D)),
-            whole((D,)),
-            whole((D, D)),
+        in_specs=[vmem, vmem, hbm, hbm, hbm],
+        out_specs=hbm,
+        out_shape=jax.ShapeDtypeStruct((rows, D), BF16),
+        scratch_shapes=[
+            pltpu.VMEM((rows, D), F32),
+            pltpu.VMEM((VOCAB, D), BF16),
+            pltpu.VMEM((D, D), BF16),
+            pltpu.VMEM((rows, D), BF16),
+            pltpu.VMEM((rows, D), BF16),
+            pltpu.SemaphoreType.DMA((2 + 2 * (rows // SUB),)),
         ],
-        out_specs=pl.BlockSpec((SUB, D), lambda g: (g, 0)),
-        out_shape=jax.ShapeDtypeStruct((rows, D), BF16),
         compiler_params=pltpu.CompilerParams(vmem_limit_bytes=60 * MIB),
         cost_estimate=pl.CostEstimate(
             flops=2 * rows * (ROWS + D) * D, bytes_accessed=8 * MIB, transcendentals=0
         ),
         name="mid",
-    )(ids, att, embed, mask_embed, wout)
+    )(ids, mask_embed, embed, wout, att)
 
 
 def coarse_kernel(q, kv, out):

time: 76.8 us -> 76.8 us (level)
  transfers between devices with their start and end apart: 3 -> 3, of which waited for: 3 -> 3; matrix products, arithmetic and copies ran while one was open for 0% -> 0% of each run, Pallas kernels for 10% -> 9%
where the time goes in v8:
time: 76.8 us; the launch traced here: 76.4 us
  Pallas kernels  33.4 us (43%)
  blocking collectives  22.3 us (29%)
  starting transfers between devices  13.4 us (17%)
  waiting for transfers between devices  4.64 us (6%)
  local copies, waits for them, and re-layouts  1.94 us (3%)
    pallas_call x1, Pallas kernels, local_attention(): pl.pallas_call(local_kernel, grid=(steps,), in_specs=[whole(x.shape) for...  22.9 us
    all_to_all x1, blocking collectives, body(): lax.all_to_all(payload, PLANE, split_axis=0, concat_axis=0, tiled=True)  11.2 us
    all_to_all x1, blocking collectives, body(): back = lax.all_to_all(mixed, PLANE, split_axis=0, concat_axis=0, tiled=True)  11.1 us
    ppermute x1, starting transfers between devices, body(): high = lax.ppermute(jnp.where(here == 0, 0, own[:HALF_WIN]), ALL, backward)  8.27 us
    pallas_call x1, Pallas kernels, make_mid(): pl.pallas_call(mid_kernel, in_specs=[vmem, vmem, hbm, hbm, hbm], out_spec...  6.99 us
    all_to_all x1, starting transfers between devices, body(): kv = lax.all_to_all(kv, RING, split_axis=0, concat_axis=0, tiled=True)  5.06 us
    all_to_all x1, waiting for transfers between devices, body(): kv = lax.all_to_all(kv, RING, split_axis=0, concat_axis=0, tiled=True)  3.34 us
    pallas_call x1, Pallas kernels, finish(): pl.pallas_call(final_kernel, grid=(rows // SUB,), in_specs=[whole(back.sh...  2.37 us
  transfers between devices with their start and end apart: 3, of which 3 were waited for; matrix products, arithmetic and copies ran while one was open for 0% of the time, Pallas kernels for 9%

profile of v8, /device:TPU:0, one launch (start us, length us, event | category | flops | bytes accessed | tf_op | source)
XLA Modules:
  0.0 76.4 jit_solution(17249389093322700057)
XLA Ops:
  0.0 0.7 add_select_fusion.own.ids
  0.7 0.0 copy-start.2
  0.7 0.1 collective-permute-start
  0.8 8.3 %collective-permute-start.1 = (s32[512]{0:T(512)S(1)}, s32[512]{0:T(512)S(1)}, u32[]{:S(2)}, u32[]{:S(2)}) collective-permute-start(s32[512]{0:T(512)S(1)} %get-tuple-element.13), channel_id=1, source_target_pairs={{1,0},{2,1},{3,2},{4,3},{5,4},{6,5},{7,6},{8,7},{9,8},{10,9},{11,1... | collective-permute-start | bytes 6152 | tf_op jit(solution)/shard_map/ppermute | solution.py:425
  9.1 1.2 %collective-permute-done.low = s32[512]{0:T(512)S(1)} collective-permute-done((s32[512]{0:T(512)S(1)}, s32[512]{0:T(512)S(1)}, u32[]{:S(2)}, u32[]{:S(2)}) %collective-permute-start) | collective-permute-done | bytes 2080 | tf_op jit(solution)/shard_map/ppermute | solution.py:424
  10.3 0.0 copy-start.3
  10.3 0.1 collective-permute-done.1.high
  10.4 0.0 copy-done.2
  10.4 0.5 copy-done.3
  10.8 0.0 copy-start.4
  10.8 0.6 copy-done.4
  11.4 22.9 %local.1 = (bf16[1024,1024]{1,0:T(8,128)(2,1)}, bf16[16,24,128]{2,1,0:T(8,128)(2,1)}) custom-call(s32[512]{0:T(512)} %copy-done.3, s32[1024]{0:T(1024)} %copy-done.2, s32[512]{0:T(512)} %copy-done.4, bf16[1024]{0:T(1024)(128)(2,1)} %mask_embed.3, bf16[1024]{0:T(1024)(128)(2,1)} %gain.1, bf16[1024]{0:T(1024)(128)(2,1)} %cgain.1, bf16[512,1024]{1,0:T(8,128)(2,1)} %embed_hbm.3, ...), custom_call_target="tpu_custom_call" | custom-call | flops 8858370048 | bytes 20971520 | tf_op jit(solution)/shard_map/local/pallas_call | solution.py:235
  34.4 11.2 %all_to_all.15 = bf16[16,24,128]{2,1,0:T(8,128)(2,1)S(1)} all-to-all(bf16[16,24,128]{2,1,0:T(8,128)(2,1)} %get-tuple-element.9), channel_id=1, replica_groups=mesh['x_hi'=2,'x_lo'=2,'y_hi'=2,'z_hi'=2,'z_lo'=2,'y_lo'=2,'core'=2] {'x..., dimensions={0} | all-to-all | bytes 196608 | tf_op jit(solution)/shard_map/all_to_all | solution.py:430
  45.6 0.9 %broadcast_in_dim.19 = bf16[8,256,128]{2,1,0:T(8,128)(2,1)} broadcast(bf16[256,128]{1,0:T(8,128)(2,1)S(1)} %bitcast.3), dimensions={1,2} | broadcast | bytes 589824 | tf_op jit(solution)/shard_map/broadcast_in_dim | solution.py:434
  46.4 5.1 %all-to-all-start.1 = ((bf16[8,256,128]{2,1,0:T(8,128)(2,1)}), bf16[8,256,128]{2,1,0:T(8,128)(2,1)S(1)}, u32[]{:S(2)}, u32[]{:S(2)}) async-start(bf16[8,256,128]{2,1,0:T(8,128)(2,1)} %broadcast_in_dim.19), calls=%async_computation.1 | async-start | bytes 1048576 | tf_op jit(solution)/shard_map/all_to_all | solution.py:435
  51.5 7.0 %mid.1 = bf16[1024,1024]{1,0:T(8,128)(2,1)} custom-call(s32[1024]{0:T(1024)} %copy-done.2, bf16[1024]{0:T(1024)(128)(2,1)} %mask_embed.3, bf16[512,1024]{1,0:T(8,128)(2,1)} %embed_hbm.3, bf16[1024,1024]{1,0:T(8,128)(2,1)} %wout_hbm.3, bf16[1024,1024]{1,0:T(8,128)(2,1)} %get-tuple-element.10.att_hbm), custom_call_target="tpu_custom_call" | custom-call | flops 3254779904 | bytes 8388608 | tf_op jit(solution)/shard_map/mid/pallas_call | solution.py:311
  58.5 3.3 %all-to-all-done.1 = bf16[8,256,128]{2,1,0:T(8,128)(2,1)S(1)} async-done(((bf16[8,256,128]{2,1,0:T(8,128)(2,1)}), bf16[8,256,128]{2,1,0:T(8,128)(2,1)S(1)}, u32[]{:S(2)}, u32[]{:S(2)}) %all-to-all-start.1) | async-done | bytes 524320 | tf_op jit(solution)/shard_map/all_to_all | solution.py:435
  61.8 0.0 copy-start
  61.8 0.0 copy-start.1
  61.8 1.1 %coarse.1 = bf16[16,8,128]{2,1,0:T(8,128)(2,1)S(1)} custom-call(bf16[16,8,128]{2,1,0:T(8,128)(2,1)S(1)} %slice.16.q, bf16[2048,128]{1,0:T(8,128)(2,1)S(1)} %bitcast.2), custom_call_target="tpu_custom_call" | custom-call | flops 8000000000 | bytes 16777216 | tf_op jit(solution)/shard_map/coarse/pallas_call | solution.py:349
  62.9 11.1 %all_to_all.16.back = bf16[16,8,128]{2,1,0:T(8,128)(2,1)S(1)} all-to-all(bf16[16,8,128]{2,1,0:T(8,128)(2,1)S(1)} %coarse.1), channel_id=1, replica_groups=mesh['x_hi'=2,'x_lo'=2,'y_hi'=2,'z_hi'=2,'z_lo'=2,'y_lo'=2,'core'=2] {'x..., dimensions={0} | all-to-all | bytes 65536 | tf_op jit(solution)/shard_map/all_to_all | solution.py:439
  74.0 0.0 copy-done
  74.0 0.0 copy-done.1
  74.0 2.4 %finish.1 = bf16[1024,1024]{1,0:T(8,128)(2,1)} custom-call(bf16[16,8,128]{2,1,0:T(8,128)(2,1)S(1)} %all_to_all.16.back, bf16[1024,1024]{1,0:T(8,128)(2,1)S(1)} %copy-done, bf16[1024,1024]{1,0:T(8,128)(2,1)S(1)} %copy-done.1), custom_call_target="tpu_custom_call" | custom-call | tf_op jit(solution)/shard_map/finish/pallas_call | solution.py:386
  (3 shorter events, 0.0 us)
Async XLA Ops:
  0.7 9.7 %copy-start.2 = (s32[1024]{0:T(1024)}, s32[1024]{0:T(1024)S(1)}, u32[]{:S(2)}) copy-start(s32[1024]{0:T(1024)S(1)} %add_select_fusion.own.ids) | copy-start | bytes 12292
  0.7 9.5 %collective-permute-start = (s32[512]{0:T(512)S(1)}, s32[512]{0:T(512)S(1)}, u32[]{:S(2)}, u32[]{:S(2)}) collective-permute-start(s32[512]{0:T(512)S(1)} %get-tuple-element.14), channel_id=1, source_target_pairs={{0,1},{1,2},{2,3},{3,4},{4,5},{5,6},{6,7},{7,8},{8,9},{9,10},{10,1... | collective-permute-start | bytes 6152 | tf_op jit(solution)/shard_map/ppermute | solution.py:424
  0.8 9.6 %collective-permute-start.1 = (s32[512]{0:T(512)S(1)}, s32[512]{0:T(512)S(1)}, u32[]{:S(2)}, u32[]{:S(2)}) collective-permute-start(s32[512]{0:T(512)S(1)} %get-tuple-element.13), channel_id=1, source_target_pairs={{1,0},{2,1},{3,2},{4,3},{5,4},{6,5},{7,6},{8,7},{9,8},{10,9},{11,1... | collective-permute-start | bytes 6152 | tf_op jit(solution)/shard_map/ppermute | solution.py:425
  10.3 0.6 copy-start.3
  10.8 0.6 copy-start.4
  46.4 15.4 %all-to-all-start.1 = ((bf16[8,256,128]{2,1,0:T(8,128)(2,1)}), bf16[8,256,128]{2,1,0:T(8,128)(2,1)S(1)}, u32[]{:S(2)}, u32[]{:S(2)}) async-start(bf16[8,256,128]{2,1,0:T(8,128)(2,1)} %broadcast_in_dim.19), calls=%async_computation.1 | async-start | bytes 1048576 | tf_op jit(solution)/shard_map/all_to_all | solution.py:435
  61.8 12.2 %copy-start = (bf16[1024,1024]{1,0:T(8,128)(2,1)S(1)}, bf16[1024,1024]{1,0:T(8,128)(2,1)}, u32[]{:S(2)}) copy-start(bf16[1024,1024]{1,0:T(8,128)(2,1)} %wout.1) | copy-start | bytes 6291460
  61.8 12.2 %copy-start.1 = (bf16[1024,1024]{1,0:T(8,128)(2,1)S(1)}, bf16[1024,1024]{1,0:T(8,128)(2,1)}, u32[]{:S(2)}) copy-start(bf16[1024,1024]{1,0:T(8,128)(2,1)} %mid.1) | copy-start | bytes 6291460
